TPU v7x, 512 devices: a whole 4x4x16 slice. The times are simulated.
512 devices in a mesh: dp: 16 (over z), expert: 32 (over x, y, core).
Axes of the slice: x: 4, y: 4, z: 16, core: 2. Of those that a mesh axis runs over, the one named last changes fastest.
Arguments:
- tokens: bfloat16 [65536, 2048], P(('dp', 'expert')), may hold values from -6 to 6
- route_gates: float32 [65536, 3], P(('dp', 'expert')), may hold values from 0.1 to 1
- expert_ids: int32 [65536, 3], P(('dp', 'expert')), may hold values from 0 to 31, all different within a row; in each aligned block of 128 rows (0 to 127, 128 to 255, ...) at most 14 rows name the same one
- owner_now: int32 [32], replicated, may hold values from 0 to 31, as said below
- owner_next: int32 [32], replicated, may hold values from 0 to 31, as said below
- out_grad: bfloat16 [65536, 2048], P(('dp', 'expert')), may hold values from -6 to 6
- expert_weights: bfloat16 [32, 2048, 1152], P('expert', 'dp'), may hold values from -0.125 to 0.125
- first_moment: bfloat16 [32, 2048, 1152], P('expert', 'dp'), may hold values from -12 to 12
- second_moment: bfloat16 [32, 2048, 1152], P('expert', 'dp'), may hold values from 5 to 80
Outputs:
- moe_out: bfloat16 [65536, 2048], P(('dp', 'expert'))
- tokens_grad: bfloat16 [65536, 2048], P(('dp', 'expert'))
- gate_grads: float32 [65536, 3], P(('dp', 'expert'))
- new_weights: bfloat16 [32, 2048, 1152], P('expert', 'dp')
- new_first: bfloat16 [32, 2048, 1152], P('expert', 'dp')
- new_second: bfloat16 [32, 2048, 1152], P('expert', 'dp')
Inputs may be any that keep to these rules, and one draw needn't show every extreme that they name: `expert_ids`: within the 128 tokens of one device no expert is named by more than 14 routes, and in some such block one expert is named by exactly 14. `owner_now`: A permutation of the 32 indices of expert. `owner_next`: A permutation that equals owner_now except on 16 experts, which exchange their holders among themselves, none keeping its own.
All inputs are finite; a program needn't handle non-finite values.
Results may differ from a plain program's by a relative error of at most 0.007.
Values may be sent and summed in bfloat16 or wider, within the bound.
A program may use at most 64 MiB of HBM per device.

v0:
```python
import jax
import jax.numpy as jnp
from jax import lax
from jax.sharding import PartitionSpec as P

beta_one = 0.9
beta_two = 0.95
learn_rate = 0.003
adam_eps = 1e-08


def route_slots(expert_ids, owner_now, capacity):
    tok_count, routes = expert_ids.shape
    experts = owner_now.shape[0]
    one_hot = (
        expert_ids[:, :, None] == jnp.arange(experts, dtype=jnp.int32)[None, None, :]
    ).astype(jnp.int32)
    slot_index = jnp.sum(one_hot * owner_now[None, None, :], axis=2)
    flat_hits = one_hot.reshape(tok_count * routes, experts)
    earlier = jnp.cumsum(flat_hits, axis=0, dtype=jnp.int32) - flat_hits
    position = jnp.sum(earlier * flat_hits, axis=1).reshape(tok_count, routes)
    return slot_index * capacity + position


def slot_rows(destination, route_gates, slot_total):
    tok_count, routes = destination.shape
    matches = (
        destination.reshape(1, tok_count * routes)
        == jnp.arange(slot_total, dtype=jnp.int32)[:, None]
    )
    token_of = (jnp.arange(tok_count * routes, dtype=jnp.int32) // routes)[None, :]
    row_token = jnp.sum(jnp.where(matches, token_of, 0), axis=1)
    row_live = jnp.any(matches, axis=1)
    row_gate = jnp.sum(jnp.where(matches, route_gates.reshape(1, -1), 0.0), axis=1)
    return (row_token, row_live, row_gate)


def owner_sources(owner_now, owner_next):
    experts = owner_now.shape[0]
    matches = owner_next[None, :] == jnp.arange(experts, dtype=jnp.int32)[:, None]
    return jnp.sum(jnp.where(matches, owner_now[None, :], 0), axis=1)


def move_late(state_block, source):
    experts = lax.axis_size("expert")
    pieces = lax.all_to_all(
        state_block.reshape(experts, -1), "expert", split_axis=0, concat_axis=0, tiled=True
    )
    return lax.all_to_all(
        pieces[source], "expert", split_axis=0, concat_axis=0, tiled=True
    ).reshape(state_block.shape)


def shards(
    tokens,
    route_gates,
    expert_ids,
    owner_now,
    owner_next,
    out_grad,
    expert_weights,
    first_moment,
    second_moment,
):
    experts = lax.axis_size("expert")
    groups = lax.axis_size("dp")
    tok_count, routes = expert_ids.shape
    model_width = tokens.shape[1]
    capacity = tok_count * routes // experts + 2
    slot_total = experts * capacity
    hidden = expert_weights.shape[2] // 3
    destination = route_slots(expert_ids, owner_now, capacity)
    row_token, row_live, row_gate = slot_rows(destination, route_gates, slot_total)
    source = owner_sources(owner_now, owner_next)
    full_weights = lax.all_gather(expert_weights[0], "dp", axis=0, tiled=True)
    weight_in = full_weights[:, : 2 * hidden]
    weight_down = full_weights[:, 2 * hidden :]
    sent_rows = jnp.where(row_live[:, None], tokens[row_token], 0).reshape(
        experts, capacity, model_width
    )
    received = lax.all_to_all(sent_rows, "expert", split_axis=0, concat_axis=0, tiled=True)
    row_inputs = received.reshape(-1, model_width)
    gate_up = jnp.dot(row_inputs, weight_in, preferred_element_type=jnp.float32)
    gate_part = gate_up[:, :hidden]
    up_part = gate_up[:, hidden:]
    activation = (gate_part * jax.nn.sigmoid(gate_part) * up_part).astype(jnp.bfloat16)
    routed = lax.dot_general(
        activation, weight_down, (((1,), (1,)), ((), ())), preferred_element_type=jnp.float32
    ).astype(jnp.bfloat16)
    returned_out = lax.all_to_all(
        routed.reshape(received.shape), "expert", split_axis=0, concat_axis=0, tiled=True
    )
    kept_gate_up = gate_up.reshape(received.shape[0], received.shape[1], 2 * hidden)
    kept_act = activation.reshape(received.shape[0], received.shape[1], hidden)
    returned_out, kept_rows, kept_gate_up, kept_act = (
        returned_out,
        received,
        kept_gate_up,
        kept_act,
    )
    picked = returned_out.reshape(slot_total, model_width)[destination].astype(jnp.float32)
    moe_out = jnp.sum(route_gates[:, :, None] * picked, axis=1).astype(jnp.bfloat16)
    gate_grads = jnp.sum(picked * out_grad.astype(jnp.float32)[:, None, :], axis=2)
    scaled = out_grad[row_token].astype(jnp.float32) * row_gate[:, None]
    route_grad = jnp.where(row_live[:, None], scaled, 0.0).astype(jnp.bfloat16)
    arrived = lax.all_to_all(
        route_grad.reshape(experts, capacity, model_width),
        "expert",
        split_axis=0,
        concat_axis=0,
        tiled=True,
    ).reshape(slot_total, model_width)
    gate_up = kept_gate_up.reshape(slot_total, 2 * hidden)
    gate_part = gate_up[:, :hidden]
    up_part = gate_up[:, hidden:]
    sigmoid_gate = jax.nn.sigmoid(gate_part)
    activation = kept_act.reshape(slot_total, hidden)
    row_inputs = kept_rows.reshape(slot_total, model_width)
    act_grad = jnp.dot(arrived, weight_down, preferred_element_type=jnp.float32)
    pre_grad = jnp.concatenate(
        [
            act_grad * up_part * sigmoid_gate * (1.0 + gate_part * (1.0 - sigmoid_gate)),
            act_grad * (gate_part * sigmoid_gate),
        ],
        axis=1,
    ).astype(jnp.bfloat16)
    input_rows = lax.dot_general(
        pre_grad, weight_in, (((1,), (1,)), ((), ())), preferred_element_type=jnp.float32
    ).astype(jnp.bfloat16)
    returned_dx = lax.all_to_all(
        input_rows.reshape(experts, capacity, model_width),
        "expert",
        split_axis=0,
        concat_axis=0,
        tiled=True,
    ).reshape(slot_total, model_width)
    tokens_grad = jnp.sum(returned_dx[destination].astype(jnp.float32), axis=1).astype(jnp.bfloat16)
    grad_in = lax.dot_general(
        row_inputs, pre_grad, (((0,), (0,)), ((), ())), preferred_element_type=jnp.float32
    )
    grad_down = lax.dot_general(
        arrived, activation, (((0,), (0,)), ((), ())), preferred_element_type=jnp.float32
    )
    partial_value = jnp.concatenate([grad_in, grad_down], axis=1).astype(jnp.bfloat16)
    partial_value = partial_value.reshape(groups, model_width // groups, 3 * hidden)
    gathered_grad = lax.all_to_all(partial_value, "dp", split_axis=0, concat_axis=0, tiled=True)
    weight_grad = jnp.sum(gathered_grad.astype(jnp.float32), axis=0)
    weight_old = expert_weights[0]
    first_old = first_moment[0]
    second_old = second_moment[0]
    first_new = beta_one * first_old.astype(jnp.float32) + (1.0 - beta_one) * weight_grad
    second_new = (
        beta_two * second_old.astype(jnp.float32) + (1.0 - beta_two) * weight_grad * weight_grad
    )
    weight_new = weight_old.astype(jnp.float32) - learn_rate * first_new / (
        jnp.sqrt(second_new) + adam_eps
    )
    new_block = jnp.stack(
        [
            weight_new.astype(jnp.bfloat16),
            first_new.astype(jnp.bfloat16),
            second_new.astype(jnp.bfloat16),
        ]
    )
    new_block = move_late(new_block, source)
    return (
        moe_out,
        tokens_grad,
        gate_grads,
        new_block[0][None],
        new_block[1][None],
        new_block[2][None],
    )


def solution(mesh):
    placed = (
        P(("dp", "expert"), None),
        P(("dp", "expert"), None),
        P(("dp", "expert"), None),
        P(),
        P(),
        P(("dp", "expert"), None),
        P("expert", "dp", None),
        P("expert", "dp", None),
        P("expert", "dp", None),
    )
    return jax.shard_map(
        shards,
        mesh=mesh,
        in_specs=placed,
        out_specs=(
            P(("dp", "expert"), None),
            P(("dp", "expert"), None),
            P(("dp", "expert"), None),
            P("expert", "dp", None),
            P("expert", "dp", None),
            P("expert", "dp", None),
        ),
        check_vma=False,
    )
```

profile of v0, /device:TPU:1, one launch (start us, length us, event | category | flops | bytes accessed | tf_op | source)
XLA Modules:
  0.0 476.7 jit_solution(14681044628764029175)
XLA Ops:
  18.3 4.0 select_convert_fusion
  22.3 10.5 %all-to-all-start.2 = ((bf16[32,14,2048]{2,1,0:T(8,128)(2,1)}), bf16[32,14,2048]{2,1,0:T(8,128)(2,1)S(1)}, u32[]{:S(2)}, u32[]{:S(2)}) async-start(bf16[32,14,2048]{2,1,0:T(8,128)(2,1)} %select_convert_fusion), calls=%async_computation.2 | async-start | bytes 4194304 | tf_op jit(solution)/shard_map/all_to_all | solution.py:106
  42.9 18.3 %all-to-all-done.2 = bf16[32,14,2048]{2,1,0:T(8,128)(2,1)S(1)} async-done(((bf16[32,14,2048]{2,1,0:T(8,128)(2,1)}), bf16[32,14,2048]{2,1,0:T(8,128)(2,1)S(1)}, u32[]{:S(2)}, u32[]{:S(2)}) %all-to-all-start.2) | async-done | bytes 1835040 | tf_op jit(solution)/shard_map/all_to_all | solution.py:106
  61.2 5.6 %all-to-all-start = ((bf16[32,14,2048]{2,1,0:T(8,128)(2,1)}), bf16[32,14,2048]{2,1,0:T(8,128)(2,1)}, u32[]{:S(2)}, u32[]{:S(2)}) async-start(bf16[32,14,2048]{2,1,0:T(8,128)(2,1)} %broadcast_select_fusion), calls=%async_computation | async-start | bytes 4194304 | tf_op jit(solution)/shard_map/all_to_all | solution.py:81
  68.4 26.7 %all-to-all-done = bf16[32,14,2048]{2,1,0:T(8,128)(2,1)} async-done(((bf16[32,14,2048]{2,1,0:T(8,128)(2,1)}), bf16[32,14,2048]{2,1,0:T(8,128)(2,1)}, u32[]{:S(2)}, u32[]{:S(2)}) %all-to-all-start) | async-done | bytes 1835040 | tf_op jit(solution)/shard_map/all_to_all | solution.py:81
  110.1 12.9 %all-to-all-start.4 = ((bf16[16,128,1152]{2,1,0:T(8,128)(2,1)}), bf16[16,128,1152]{2,1,0:T(8,128)(2,1)}, u32[]{:S(2)}, u32[]{:S(2)}) async-start(bf16[16,128,1152]{2,1,0:T(8,128)(2,1)} %pad_maximum_fusion), calls=%async_computation.4 | async-start | bytes 9437184 | tf_op jit(solution)/shard_map/all_to_all | solution.py:146
  128.3 199.0 %all-to-all-done.4 = bf16[16,128,1152]{2,1,0:T(8,128)(2,1)} async-done(((bf16[16,128,1152]{2,1,0:T(8,128)(2,1)}), bf16[16,128,1152]{2,1,0:T(8,128)(2,1)}, u32[]{:S(2)}, u32[]{:S(2)}) %all-to-all-start.4) | async-done | bytes 4718624 | tf_op jit(solution)/shard_map/all_to_all | solution.py:146
  327.3 5.6 %all-to-all-start.3 = ((bf16[32,14,2048]{2,1,0:T(8,128)(2,1)}), bf16[32,14,2048]{2,1,0:T(8,128)(2,1)S(1)}, u32[]{:S(2)}, u32[]{:S(2)}) async-start(bf16[32,14,2048]{2,1,0:T(8,128)(2,1)} %reshape.197), calls=%async_computation.3 | async-start | bytes 4194304 | tf_op jit(solution)/shard_map/all_to_all | solution.py:130
  337.6 5.0 %all_to_all.39 = bf16[32,1,13824]{2,1,0:T(2,128)(2,1)} reshape(bf16[3,128,1152]{2,1,0:T(8,128)(2,1)} %pad_maximum_fusion.1) | data formatting | bytes 1769472 | tf_op jit(solution)/shard_map/all_to_all | solution.py:46
  343.2 8.0 %reduce.5 = bf16[32,13824]{1,0:T(8,128)(2,1)} reduce(bf16[32,1,13824]{2,1,0:T(2,128)(2,1)} %all_to_all.39, bf16[]{:T(256)} %broadcast.184), dimensions={1}, to_apply=%all_to_all.39.reduce_sub_computation | reduce | bytes 1769474 | tf_op jit(solution)/shard_map/all_to_all | solution.py:46
  354.3 6.9 %all-to-all-done.3 = bf16[32,14,2048]{2,1,0:T(8,128)(2,1)S(1)} async-done(((bf16[32,14,2048]{2,1,0:T(8,128)(2,1)}), bf16[32,14,2048]{2,1,0:T(8,128)(2,1)S(1)}, u32[]{:S(2)}, u32[]{:S(2)}) %all-to-all-start.3) | async-done | bytes 1835040 | tf_op jit(solution)/shard_map/all_to_all | solution.py:130
  361.2 5.1 %all-to-all-start.5 = ((bf16[32,2,6912]{2,1,0:T(2,128)(2,1)}), bf16[32,2,6912]{2,1,0:T(2,128)(2,1)}, u32[]{:S(2)}, u32[]{:S(2)}) async-start(bf16[32,2,6912]{2,1,0:T(2,128)(2,1)} %reshape.249), calls=%async_computation.5 | async-start | bytes 1769472 | tf_op jit(solution)/shard_map/all_to_all | solution.py:46
  366.3 3.8 convolution_convert_fusion.1
  373.7 7.9 %all-to-all-done.5 = bf16[32,2,6912]{2,1,0:T(2,128)(2,1)} async-done(((bf16[32,2,6912]{2,1,0:T(2,128)(2,1)}), bf16[32,2,6912]{2,1,0:T(2,128)(2,1)}, u32[]{:S(2)}, u32[]{:S(2)}) %all-to-all-start.5) | async-done | bytes 884768 | tf_op jit(solution)/shard_map/all_to_all | solution.py:46
  381.6 4.7 all-to-all-start.1
  386.5 6.0 %reshape.250 = bf16[32,1,13824]{2,1,0:T(2,128)(2,1)} reshape(bf16[32,2,6912]{2,1,0:T(2,128)(2,1)} %all-to-all-done.5) | data formatting | bytes 1769472
  397.7 16.9 %all-to-all-done.1 = bf16[32,14,2048]{2,1,0:T(8,128)(2,1)} async-done(((bf16[32,14,2048]{2,1,0:T(8,128)(2,1)}), bf16[32,14,2048]{2,1,0:T(8,128)(2,1)}, u32[]{:S(2)}, u32[]{:S(2)}) %all-to-all-start.1) | async-done | bytes 1835040 | tf_op jit(solution)/shard_map/all_to_all | solution.py:90
  414.5 5.1 %all-to-all-start.6 = ((bf16[32,2,6912]{2,1,0:T(2,128)(2,1)}), bf16[32,2,6912]{2,1,0:T(2,128)(2,1)}, u32[]{:S(2)}, u32[]{:S(2)}) async-start(bf16[32,2,6912]{2,1,0:T(2,128)(2,1)} %reshape.251), calls=%async_computation.6 | async-start | bytes 1769472 | tf_op jit(solution)/shard_map/all_to_all | solution.py:49
  427.1 5.2 %reshape.230 = bf16[128,3,2048]{2,1,0:T(4,128)(2,1)} reshape(bf16[384,2048]{1,0:T(8,128)(2,1)} %gather_fusion.3) | data formatting | bytes 3145728 | tf_op jit(solution)/shard_map/gather | solution.py:137
  437.9 5.6 %reshape.244 = f32[128,3,2048]{2,1,0:T(4,128)} reshape(bf16[384,2048]{1,0:T(8,128)(2,1)} %gather_fusion.1) | data formatting | bytes 4718592 | tf_op jit(solution)/shard_map/convert_element_type | solution.py:101
  443.5 6.7 %multiply_reduce_fusion = (f32[128,3]{1,0:T(8,128)S(1)}, bf16[128,2048]{1,0:T(8,128)(2,1)}) fusion(f32[128,3,2048]{2,1,0:T(4,128)} %reshape.244, f32[128,2048]{1,0:T(8,128)S(1)} %copy-done.6, f32[128,3]{1,0:T(8,128)S(1)} %copy.46), kind=kLoop, calls=%fused_computation.7 | loop fusion | flops 2883200 | bytes 4721664 | tf_op jit(solution)/shard_map/reduce_sum | solution.py:103
  450.8 3.9 reduce_sum.96
  454.7 5.3 %reshape.252 = bf16[32,1,13824]{2,1,0:T(2,128)(2,1)S(1)} reshape(bf16[32,2,6912]{2,1,0:T(2,128)(2,1)} %all-to-all-done.6) | data formatting | bytes 1769472
  460.0 6.2 %reduce.3 = bf16[32,13824]{1,0:T(8,128)(2,1)} reduce(bf16[32,1,13824]{2,1,0:T(2,128)(2,1)S(1)} %reshape.252, bf16[]{:T(256)} %constant.57), dimensions={1}, to_apply=%all_to_all.38.reduce_sub_computation | reduce | bytes 1769474 | tf_op jit(solution)/shard_map/all_to_all | solution.py:49
  (104 shorter events, 77.3 us)
Async XLA Ops:
  7.2 25.7 %copy-start = (bf16[128,2048]{1,0:T(8,128)(2,1)S(1)}, bf16[128,2048]{1,0:T(8,128)(2,1)}, u32[]{:S(2)}) copy-start(bf16[128,2048]{1,0:T(8,128)(2,1)} %param.9) | copy-start | bytes 1572868
  7.2 5.5 %copy-start.2 = (bf16[128,2048]{1,0:T(8,128)(2,1)S(1)}, bf16[128,2048]{1,0:T(8,128)(2,1)}, u32[]{:S(2)}) copy-start(bf16[128,2048]{1,0:T(8,128)(2,1)} %param.14) | copy-start | bytes 1572868
  7.2 90.4 %all-gather.3.cloned.1.call-start = ((), (), s32[]{:S(2)}) async-start(), calls=%async_computation.7 | async-start | bytes 5013504 | tf_op jit(solution)/shard_map/all_gather | solution.py:75
  15.2 2.3 copy-start.14
  22.3 38.9 %all-to-all-start.2 = ((bf16[32,14,2048]{2,1,0:T(8,128)(2,1)}), bf16[32,14,2048]{2,1,0:T(8,128)(2,1)S(1)}, u32[]{:S(2)}, u32[]{:S(2)}) async-start(bf16[32,14,2048]{2,1,0:T(8,128)(2,1)} %select_convert_fusion), calls=%async_computation.2 | async-start | bytes 4194304 | tf_op jit(solution)/shard_map/all_to_all | solution.py:106
  61.2 33.8 %all-to-all-start = ((bf16[32,14,2048]{2,1,0:T(8,128)(2,1)}), bf16[32,14,2048]{2,1,0:T(8,128)(2,1)}, u32[]{:S(2)}, u32[]{:S(2)}) async-start(bf16[32,14,2048]{2,1,0:T(8,128)(2,1)} %broadcast_select_fusion), calls=%async_computation | async-start | bytes 4194304 | tf_op jit(solution)/shard_map/all_to_all | solution.py:81
  97.6 3.6 copy-start.5
  104.0 3.2 copy-start.17
  110.1 217.2 %all-to-all-start.4 = ((bf16[16,128,1152]{2,1,0:T(8,128)(2,1)}), bf16[16,128,1152]{2,1,0:T(8,128)(2,1)}, u32[]{:S(2)}, u32[]{:S(2)}) async-start(bf16[16,128,1152]{2,1,0:T(8,128)(2,1)} %pad_maximum_fusion), calls=%async_computation.4 | async-start | bytes 9437184 | tf_op jit(solution)/shard_map/all_to_all | solution.py:146
  327.3 33.9 %all-to-all-start.3 = ((bf16[32,14,2048]{2,1,0:T(8,128)(2,1)}), bf16[32,14,2048]{2,1,0:T(8,128)(2,1)S(1)}, u32[]{:S(2)}, u32[]{:S(2)}) async-start(bf16[32,14,2048]{2,1,0:T(8,128)(2,1)} %reshape.197), calls=%async_computation.3 | async-start | bytes 4194304 | tf_op jit(solution)/shard_map/all_to_all | solution.py:130
  332.9 3.2 copy-start.7
  332.9 3.2 copy-start.8
  332.9 3.2 copy-start.9
  361.2 8.9 %copy-start.4 = (bf16[32,14,2048]{2,1,0:T(8,128)(2,1)}, bf16[32,14,2048]{2,1,0:T(8,128)(2,1)S(1)}, u32[]{:S(2)}) copy-start(bf16[32,14,2048]{2,1,0:T(8,128)(2,1)S(1)} %all-to-all-done.3) | copy-start | bytes 5505028
  361.2 20.4 %all-to-all-start.5 = ((bf16[32,2,6912]{2,1,0:T(2,128)(2,1)}), bf16[32,2,6912]{2,1,0:T(2,128)(2,1)}, u32[]{:S(2)}, u32[]{:S(2)}) async-start(bf16[32,2,6912]{2,1,0:T(2,128)(2,1)} %reshape.249), calls=%async_computation.5 | async-start | bytes 1769472 | tf_op jit(solution)/shard_map/all_to_all | solution.py:46
  373.7 12.6 %copy-start.15 = (s32[32]{0:T(128)S(1)}, s32[32]{0:T(128)}, u32[]{:S(2)}) copy-start(s32[32]{0:T(128)} %param.12) | copy-start | bytes 388
  373.7 12.6 %copy-start.16 = (s32[32]{0:T(128)S(1)}, s32[32]{0:T(128)}, u32[]{:S(2)}) copy-start(s32[32]{0:T(128)} %param.13) | copy-start | bytes 388
  381.6 33.0 %all-to-all-start.1 = ((bf16[32,14,2048]{2,1,0:T(8,128)(2,1)}), bf16[32,14,2048]{2,1,0:T(8,128)(2,1)}, u32[]{:S(2)}, u32[]{:S(2)}) async-start(bf16[32,14,2048]{2,1,0:T(8,128)(2,1)} %reshape.193), calls=%async_computation.1 | async-start | bytes 4194304 | tf_op jit(solution)/shard_map/all_to_all | solution.py:90
  396.5 23.2 %copy-start.11 = (s32[384]{0:T(512)S(1)}, s32[384]{0:T(512)}, u32[]{:S(2)}) copy-start(s32[384]{0:T(512)} %copy-done.10) | copy-start | bytes 4612
  397.7 23.4 %copy-start.13 = (s32[128,3]{0,1:T(4,128)S(1)}, s32[128,3]{0,1:T(4,128)}, u32[]{:S(2)}) copy-start(s32[128,3]{0,1:T(4,128)} %copy-done.12) | copy-start | bytes 4612
  414.5 40.2 %all-to-all-start.6 = ((bf16[32,2,6912]{2,1,0:T(2,128)(2,1)}), bf16[32,2,6912]{2,1,0:T(2,128)(2,1)}, u32[]{:S(2)}, u32[]{:S(2)}) async-start(bf16[32,2,6912]{2,1,0:T(2,128)(2,1)} %reshape.251), calls=%async_computation.6 | async-start | bytes 1769472 | tf_op jit(solution)/shard_map/all_to_all | solution.py:49
  437.9 5.6 %copy-start.6 = (f32[128,2048]{1,0:T(8,128)S(1)}, f32[128,2048]{1,0:T(8,128)}, u32[]{:S(2)}) copy-start(f32[128,2048]{1,0:T(8,128)} %convert_element_type.83) | copy-start | bytes 3145732
  443.5 7.3 %copy-start.3 = (bf16[128,3,2048]{2,1,0:T(4,128)(2,1)S(1)}, bf16[128,3,2048]{2,1,0:T(4,128)(2,1)}, u32[]{:S(2)}) copy-start(bf16[128,3,2048]{2,1,0:T(4,128)(2,1)} %reshape.230) | copy-start | bytes 4718596
  460.0 9.7 %copy-start.1 = (bf16[128,2048]{1,0:T(8,128)(2,1)S(1)}, bf16[128,2048]{1,0:T(8,128)(2,1)}, u32[]{:S(2)}) copy-start(bf16[128,2048]{1,0:T(8,128)(2,1)} %param.9) | copy-start | bytes 1572868
  (2 other events, 1.2 us)
Sparse Core Ops, SparseCore 0:
  10.1 77.4 all-gather.2
where the time goes:
time: 484 us; the launch traced here: 477 us
  waiting for transfers between devices  276 us (57%)
  local copies, waits for them, and re-layouts  74.7 us (15%)
  starting transfers between devices  49.7 us (10%)
  other arithmetic  44.4 us (9%)
  matrix products  17 us (4%)
  between operations  14.7 us (3%)
    all_to_all x1, waiting for transfers between devices, shards(): lax.all_to_all(partial_value, 'dp', split_axis=0, concat_axis=0, tiled=True)  199 us
    all_to_all x1, waiting for transfers between devices, shards(): lax.all_to_all(sent_rows, 'expert', split_axis=0, concat_axis=0, tiled=True)  26.7 us
    unnamed x44, local copies, waits for them, and re-layouts  19.7 us
    all_to_all x1, waiting for transfers between devices, shards(): lax.all_to_all(route_grad.reshape(experts, capacity, model_width), 'exper...  18.3 us
    all_to_all x1, waiting for transfers between devices, shards(): lax.all_to_all(routed.reshape(received.shape), 'expert', split_axis=0, co...  16.9 us
    all_to_all x1, starting transfers between devices, shards(): lax.all_to_all(partial_value, 'dp', split_axis=0, concat_axis=0, tiled=True)  12.9 us
    all_to_all x1, starting transfers between devices, shards(): lax.all_to_all(route_grad.reshape(experts, capacity, model_width), 'exper...  10.5 us
  transfers between devices with their start and end apart: 8, of which 6 were waited for; matrix products, arithmetic and copies ran while one was open for 22% of the time, Pallas kernels for 0%

commit v1 on v0

v1 whole, which is shorter than its diff:
```python
import functools

import jax
import jax.numpy as jnp
from jax import lax
from jax.experimental import pallas as pl
from jax.experimental.pallas import tpu as pltpu
from jax.sharding import PartitionSpec as P

MESH = pl.DeviceIdType.MESH
BF16 = jnp.bfloat16
F32 = jnp.float32

beta_one = 0.9
beta_two = 0.95
learn_rate = 0.003
adam_eps = 1e-08

SLOT = 16
WIDE, NARROW = 256, 128
CHUNKS = 2


def dot(a, b, dims):
    return lax.dot_general(a, b, (dims, ((), ())), preferred_element_type=F32)


def kernel(
    cfg,
    source,
    tokens,
    gates,
    ids,
    owner_next,
    out_grad,
    w_old,
    m_old,
    v_old,
    moe_out,
    tokens_grad,
    gate_grads,
    w_new,
    m_new,
    v_new,
    x_send,
    g_send,
    x_in,
    g_in,
    weights,
    gate_up,
    act,
    pre,
    ro_send,
    dx_send,
    ro_in,
    dx_in,
    sum_send,
    sum_in,
    part,
    place,
    place_gate,
    hop_w_a,
    hop_m_a,
    hop_v_a,
    hop_w_b,
    hop_m_b,
    hop_v_b,
    out_a,
    out_b,
    moments,
    a2a_s,
    a2a_r,
    hop1_s,
    hop1_r,
    hop2_s,
    hop2_r,
    ag_s,
    ag_r,
    rs_s,
    rs_r,
):
    groups, experts, xs, ys = cfg
    hop_a, hop_b = (hop_w_a, hop_m_a, hop_v_a), (hop_w_b, hop_m_b, hop_v_b)
    dp = lax.axis_index("dp")
    me = lax.axis_index("expert")
    tok, width = tokens.shape
    rows, cols = w_old.shape
    hid = cols // 3
    slots = experts * SLOT
    n_wide = cols // WIDE
    n_row = rows // SLOT
    n_right = groups // 2
    n_left = groups - 1 - n_right
    part_rows = rows // CHUNKS
    right = lax.rem(dp + 1, groups)
    left = lax.rem(dp + groups - 1, groups)
    my_x, my_y, my_c = me // (2 * ys), (me // 2) % ys, me % 2

    def peer(i):
        off = (i * 11) % experts
        px = (my_x + off // (2 * ys)) % xs
        py = (my_y + (off // 2) % ys) % ys
        return (px * ys + py) * 2 + (my_c + off) % 2

    def each_peer(low, high, body):
        def step(i, carry):
            body(peer(i))
            return carry

        lax.fori_loop(low, high, step, 0)

    def remote(src, dst, ssem, rsem, device):
        pltpu.make_async_remote_copy(
            src_ref=src,
            dst_ref=dst,
            send_sem=ssem,
            recv_sem=rsem,
            device_id=device,
            device_id_type=MESH,
        ).start()

    def await_bytes(ref, sem):
        pltpu.make_async_copy(ref, ref, sem).wait()

    barrier = pltpu.get_barrier_semaphore()
    each_peer(
        1,
        experts,
        lambda d: pl.semaphore_signal(
            barrier, inc=1, device_id=(dp, d), device_id_type=MESH
        ),
    )
    for z in (left, right):
        pl.semaphore_signal(barrier, inc=1, device_id=(z, me), device_id_type=MESH)
    pl.semaphore_wait(barrier, experts + 1)

    def piece(ref, relay, base=0):
        return ref.at[
            pl.ds(pl.multiple_of(base + (relay // n_wide) * SLOT, SLOT), SLOT),
            pl.ds(pl.multiple_of((relay % n_wide) * WIDE, WIDE), WIDE),
        ]

    def rest(ref, relay, base=0):
        return ref.at[
            pl.ds(pl.multiple_of(base + (relay // n_wide) * SLOT, SLOT), SLOT),
            pl.ds(n_wide * WIDE, NARROW),
        ]

    def hop_one(a, ref):
        chosen = a % n_wide

        def one(d):
            remote(piece(ref, d), hop_a[a].at[me], hop1_s.at[a, 0], hop1_r.at[a, 0], (dp, d))

            @pl.when(d % n_wide == chosen)
            def _():
                remote(rest(ref, d), hop_b[a].at[me], hop1_s.at[a, 1], hop1_r.at[a, 1], (dp, d))

        each_peer(1, experts, one)
        hop_a[a][me] = piece(ref, me)[...]

        @pl.when(me % n_wide == chosen)
        def _():
            hop_b[a][me] = rest(ref, me)[...]

    def hop_two(a, ref, base):
        chosen = a % n_wide
        await_bytes(hop_a[a].at[pl.ds(0, experts - 1)], hop1_r.at[a, 0])

        def pick_a(s, carry):
            out_a[a, s] = hop_a[a][source[s]]
            return carry

        lax.fori_loop(0, experts, pick_a, 0)
        each_peer(
            1,
            experts,
            lambda d: remote(
                out_a.at[a, d], piece(ref, me, base), hop2_s.at[a, 0], hop2_r.at[a, 0], (dp, d)
            ),
        )
        piece(ref, me, base)[...] = out_a[a, me]

        @pl.when(me % n_wide == chosen)
        def _():
            await_bytes(hop_b[a].at[pl.ds(0, experts - 1)], hop1_r.at[a, 1])

            def pick_b(s, carry):
                out_b[a, s] = hop_b[a][source[s]]
                return carry

            lax.fori_loop(0, experts, pick_b, 0)
            each_peer(
                1,
                experts,
                lambda d: remote(
                    out_b.at[a, d], rest(ref, me, base), hop2_s.at[a, 1], hop2_r.at[a, 1], (dp, d)
                ),
            )
            rest(ref, me, base)[...] = out_b[a, me]

    def narrow_wait(a, sem):
        chosen = a % n_wide

        @pl.when(me % n_wide == chosen)
        def _():
            await_bytes(hop_b[a].at[pl.ds(0, n_row - 1)], sem)

        @pl.when(me % n_wide != chosen)
        def _():
            await_bytes(hop_b[a].at[pl.ds(0, n_row)], sem)

    def arrived(a):
        await_bytes(hop_a[a].at[pl.ds(0, experts - 1)], hop2_r.at[a, 0])
        narrow_wait(a, hop2_r.at[a, 1])

    def hops_sent(a):
        await_bytes(hop_a[a].at[pl.ds(0, experts - 1)], hop1_s.at[a, 0])
        narrow_wait(a, hop1_s.at[a, 1])
        await_bytes(hop_a[a].at[pl.ds(0, experts - 1)], hop2_s.at[a, 0])

        @pl.when(me % n_wide == a % n_wide)
        def _():
            await_bytes(hop_b[a].at[pl.ds(0, experts - 1)], hop2_s.at[a, 1])

    def zone(z, ch=0, size=None):
        start = ((z + groups) % groups) * rows + ch * part_rows
        return pl.ds(pl.multiple_of(start, part_rows), size or rows)

    hop_one(0, w_old)

    lane = lax.broadcasted_iota(jnp.int32, (tok, experts), 1)
    hits = [(ids[:, r : r + 1] == lane).astype(F32) for r in range(3)]
    before = lax.broadcasted_iota(jnp.int32, (tok, tok), 1) < lax.broadcasted_iota(
        jnp.int32, (tok, tok), 0
    )
    position = dot(
        before.astype(F32).astype(BF16),
        (hits[0] + hits[1] + hits[2]).astype(BF16),
        ((1,), (0,)),
    )
    row_at = owner_next[...].astype(F32) * SLOT + position
    target = [
        jnp.sum(h * row_at, axis=1, keepdims=True).astype(jnp.int32) for h in hits
    ]
    slot_lane = lax.broadcasted_iota(jnp.int32, (tok, slots), 1)
    spread = jnp.zeros((tok, slots), F32)
    weighted = jnp.zeros((tok, slots), F32)
    for r in range(3):
        here = slot_lane == target[r]
        spread = spread + here.astype(F32)
        weighted = weighted + jnp.where(here, gates[:, r : r + 1], 0.0)
    place[...] = spread
    place_gate[...] = weighted
    rows_of = spread.T.astype(BF16)
    gate_of = jnp.sum(weighted.T, axis=1, keepdims=True)

    block = min(256, width)

    def gather(c, carry):
        at = pl.ds(pl.multiple_of(c * block, block), block)
        x_send[:, at] = dot(rows_of, tokens[:, at], ((1,), (0,))).astype(BF16)
        g_send[:, at] = (dot(rows_of, out_grad[:, at], ((1,), (0,))) * gate_of).astype(BF16)
        return carry

    lax.fori_loop(0, width // block, gather, 0)

    hop_two(0, weights, dp * rows)

    def send_rows(n, src, dst):
        def one(d):
            remote(
                src.at[pl.ds(pl.multiple_of(d * SLOT, SLOT), SLOT)],
                dst.at[pl.ds(pl.multiple_of(me * SLOT, SLOT), SLOT)],
                a2a_s.at[n],
                a2a_r.at[n],
                (dp, d),
            )

        return one

    mine = pl.ds(pl.multiple_of(me * SLOT, SLOT), SLOT)

    def dispatch(low, high):
        def both(d):
            send_rows(0, x_send, x_in)(d)
            send_rows(1, g_send, g_in)(d)

        each_peer(low, high, both)

    def rows_arrived(n, ref):
        await_bytes(ref.at[pl.ds(0, (experts - 1) * SLOT)], a2a_r.at[n])

    def share(total, steps, k):
        per = -(-total // steps)
        return 1 + jnp.minimum(k * per, total), 1 + jnp.minimum((k + 1) * per, total)

    others = experts - 1
    dispatch(*share(others, n_right, 0))
    x_in[mine, :] = x_send[mine, :]
    g_in[mine, :] = g_send[mine, :]

    def gather_copy(way, k, ch):
        at = zone(dp - k if way == 0 else dp + k, ch, part_rows)
        remote(
            weights.at[at],
            weights.at[at],
            ag_s.at[way, k, ch],
            ag_r.at[way, k, ch],
            (right if way == 0 else left, me),
        )

    arrived(0)
    for ch in range(CHUNKS):
        gather_copy(0, 0, ch)
        if n_left:
            gather_copy(1, 0, ch)

    def gather_step(k, carry):
        for ch in range(CHUNKS):
            for way, count in ((0, n_right), (1, n_left)):

                @pl.when(k < count)
                def _():
                    z = dp - k - 1 if way == 0 else dp + k + 1
                    await_bytes(weights.at[zone(z, ch, part_rows)], ag_r.at[way, k, ch])

                @pl.when(k + 1 < count)
                def _():
                    gather_copy(way, k + 1, ch)

        @pl.when(k + 1 < n_right)
        def _():
            dispatch(*share(others, n_right, k + 1))

        return carry

    lax.fori_loop(0, n_right, gather_step, 0)

    hop_one(1, m_old)
    hop_one(2, v_old)

    rows_arrived(0, x_in)
    rows_arrived(1, g_in)
    for c in range(0, 3 * hid, min(256, hid)):
        n = min(256, hid)
        if c < 2 * hid:
            gate_up[:, c : c + n] = dot(x_in[...], weights[:, c : c + n], ((1,), (0,)))
    for c in range(0, hid, 128):
        gate_up[:, 2 * hid + c : 2 * hid + c + 128] = dot(
            g_in[...], weights[:, 2 * hid + c : 2 * hid + c + 128], ((1,), (0,))
        )

    height = min(64, slots)

    def hidden(c, carry):
        at = pl.ds(pl.multiple_of(c * height, height), height)
        gate = gate_up[at, 0:hid]
        up = gate_up[at, hid : 2 * hid]
        grad = gate_up[at, 2 * hid : 3 * hid]
        sig = jax.nn.sigmoid(gate)
        act[at, :] = (gate * sig * up).astype(BF16)
        pre[at, 0:hid] = (grad * up * sig * (1.0 + gate * (1.0 - sig))).astype(BF16)
        pre[at, hid : 2 * hid] = (grad * (gate * sig)).astype(BF16)
        return carry

    lax.fori_loop(0, slots // height, hidden, 0)

    def partial(z, n):
        at = zone(z)
        part[n, :, 0 : 2 * hid] = dot(x_in[:, at], pre[...], ((0,), (0,)))
        part[n, :, 2 * hid : 3 * hid] = dot(g_in[:, at], act[...], ((0,), (0,)))

    def sum_copy(way, k, ch):
        at = pl.ds(ch * part_rows, part_rows)
        remote(
            sum_send.at[way, k, at],
            sum_in.at[way, k, at],
            rs_s.at[way, k, ch],
            rs_r.at[way, k, ch],
            (right if way == 0 else left, me),
        )

    def sum_arrived(way, k, ch):
        at = pl.ds(ch * part_rows, part_rows)
        await_bytes(sum_in.at[way, k, at], rs_r.at[way, k, ch])

    for way, count, z in ((0, n_right, dp + n_right), (1, n_left, dp - n_left)):
        if count:
            partial(z, way)
            sum_send[way, 0] = part[way].astype(BF16)
            for ch in range(CHUNKS):
                sum_copy(way, 0, ch)

    hop_two(1, moments.at[0], 0)
    hop_two(2, moments.at[1], 0)

    def route_out(c, carry):
        at = pl.ds(pl.multiple_of(c * block, block), block)
        ro_send[:, at] = dot(act[...], weights[at, 2 * hid : 3 * hid], ((1,), (1,))).astype(BF16)
        dx_send[:, at] = dot(pre[...], weights[at, 0 : 2 * hid], ((1,), (1,))).astype(BF16)
        return carry

    lax.fori_loop(0, width // block, route_out, 0)

    def give_back(low, high):
        def both(d):
            send_rows(2, ro_send, ro_in)(d)
            send_rows(3, dx_send, dx_in)(d)

        each_peer(low, high, both)

    give_back(*share(others, 4, 0))
    ro_in[mine, :] = ro_send[mine, :]
    dx_in[mine, :] = dx_send[mine, :]

    def sum_step(k, carry):
        partial(dp + n_right - k, 0)

        @pl.when(k < n_left)
        def _():
            partial(dp - n_left + k, 1)

        for ch in range(CHUNKS):
            at = pl.ds(ch * part_rows, part_rows)
            for way, count in ((0, n_right), (1, n_left)):

                @pl.when(k < count)
                def _():
                    sum_arrived(way, k - 1, ch)
                    sum_send[way, k, at] = (
                        part[way, at] + sum_in[way, k - 1, at].astype(F32)
                    ).astype(BF16)
                    sum_copy(way, k, ch)

        @pl.when(k < 4)
        def _():
            give_back(*share(others, 4, k))

        return carry

    lax.fori_loop(1, n_right, sum_step, 0)
    for k in range(n_right, 4):
        give_back(*share(others, 4, k))
    partial(dp, 0)

    rows_arrived(2, ro_in)
    gate_high = place_gate[...].astype(BF16)
    gate_low = (place_gate[...] - gate_high.astype(F32)).astype(BF16)

    def combine(c, total):
        at = pl.ds(pl.multiple_of(c * block, block), block)
        rows_here = ro_in[:, at]
        moe_out[:, at] = (
            dot(gate_high, rows_here, ((1,), (0,))) + dot(gate_low, rows_here, ((1,), (0,)))
        ).astype(BF16)
        return total + dot(out_grad[:, at], rows_here, ((1,), (1,)))

    products = lax.fori_loop(0, width // block, combine, jnp.zeros((tok, slots), F32))
    for r in range(3):
        gate_grads[:, r : r + 1] = jnp.sum(
            jnp.where(slot_lane == target[r], products, 0.0), axis=1, keepdims=True
        )
    rows_arrived(3, dx_in)
    spread_low = place[...].astype(BF16)

    def combine_dx(c, carry):
        at = pl.ds(pl.multiple_of(c * block, block), block)
        tokens_grad[:, at] = dot(spread_low, dx_in[:, at], ((1,), (0,))).astype(BF16)
        return carry

    lax.fori_loop(0, width // block, combine_dx, 0)

    arrived(1)
    arrived(2)
    for ch in range(CHUNKS):
        sum_arrived(0, n_right - 1, ch)
        if n_left:
            sum_arrived(1, n_left - 1, ch)
    w_base = dp * rows

    def adam(c, carry):
        at = pl.ds(pl.multiple_of(c * SLOT, SLOT), SLOT)
        grad = part[0, at] + sum_in[0, n_right - 1, at].astype(F32)
        if n_left:
            grad = grad + sum_in[1, n_left - 1, at].astype(F32)
        first = beta_one * moments[0, at].astype(F32) + (1.0 - beta_one) * grad
        second = beta_two * moments[1, at].astype(F32) + (1.0 - beta_two) * grad * grad
        old = weights[pl.ds(pl.multiple_of(w_base + c * SLOT, SLOT), SLOT), :].astype(F32)
        w_new[at, :] = (old - learn_rate * first / (jnp.sqrt(second) + adam_eps)).astype(BF16)
        m_new[at, :] = first.astype(BF16)
        v_new[at, :] = second.astype(BF16)
        return carry

    lax.fori_loop(0, rows // SLOT, adam, 0)

    for n, ref in enumerate((x_send, g_send, ro_send, dx_send)):
        await_bytes(ref.at[pl.ds(0, others * SLOT)], a2a_s.at[n])
    for a in range(3):
        hops_sent(a)
    for way, count in ((0, n_right), (1, n_left)):

        def left_here(k, carry):
            for ch in range(CHUNKS):
                at = pl.ds(ch * part_rows, part_rows)
                await_bytes(sum_send.at[way, k, at], ag_s.at[way, k, ch])
                await_bytes(sum_send.at[way, k, at], rs_s.at[way, k, ch])
            return carry

        lax.fori_loop(0, count, left_here, 0)


def shards(
    grid,
    tokens,
    route_gates,
    expert_ids,
    owner_now,
    owner_next,
    out_grad,
    expert_weights,
    first_moment,
    second_moment,
):
    groups, experts = lax.axis_size("dp"), lax.axis_size("expert")
    tok, width = tokens.shape
    _, rows, cols = expert_weights.shape
    hid = cols // 3
    slots = experts * SLOT
    n_right = groups // 2
    matches = owner_next[None, :] == jnp.arange(experts, dtype=jnp.int32)[:, None]
    source = jnp.sum(jnp.where(matches, owner_now[None, :], 0), axis=1)
    vmem = pl.BlockSpec(memory_space=pltpu.VMEM)
    dma = pltpu.SemaphoreType.DMA
    state = jax.ShapeDtypeStruct((rows, cols), BF16)
    result = pl.pallas_call(
        functools.partial(kernel, (groups, experts, *grid)),
        out_shape=(
            jax.ShapeDtypeStruct((tok, width), BF16),
            jax.ShapeDtypeStruct((tok, width), BF16),
            jax.ShapeDtypeStruct(route_gates.shape, F32),
            state,
            state,
            state,
        ),
        in_specs=[pl.BlockSpec(memory_space=pltpu.SMEM)] + [vmem] * 8,
        out_specs=(vmem,) * 6,
        scratch_shapes=[
            pltpu.VMEM((slots, width), BF16),
            pltpu.VMEM((slots, width), BF16),
            pltpu.VMEM((slots, width), BF16),
            pltpu.VMEM((slots, width), BF16),
            pltpu.VMEM((width, cols), BF16),
            pltpu.VMEM((slots, cols), F32),
            pltpu.VMEM((slots, hid), BF16),
            pltpu.VMEM((slots, 2 * hid), BF16),
            pltpu.VMEM((slots, width), BF16),
            pltpu.VMEM((slots, width), BF16),
            pltpu.VMEM((slots, width), BF16),
            pltpu.VMEM((slots, width), BF16),
            pltpu.VMEM((2, n_right, rows, cols), BF16),
            pltpu.VMEM((2, n_right, rows, cols), BF16),
            pltpu.VMEM((2, rows, cols), F32),
            pltpu.VMEM((tok, slots), F32),
            pltpu.VMEM((tok, slots), F32),
            *[pltpu.VMEM((experts, SLOT, WIDE), BF16)] * 3,
            *[pltpu.VMEM((experts, SLOT, NARROW), BF16)] * 3,
            pltpu.VMEM((3, experts, SLOT, WIDE), BF16),
            pltpu.VMEM((3, experts, SLOT, NARROW), BF16),
            pltpu.VMEM((2, rows, cols), BF16),
            dma((4,)),
            dma((4,)),
            dma((3, 2)),
            dma((3, 2)),
            dma((3, 2)),
            dma((3, 2)),
            dma((2, n_right, CHUNKS)),
            dma((2, n_right, CHUNKS)),
            dma((2, n_right, CHUNKS)),
            dma((2, n_right, CHUNKS)),
        ],
        compiler_params=pltpu.CompilerParams(
            collective_id=0, has_side_effects=True, vmem_limit_bytes=60 * 2**20
        ),
        name="moe_step",
    )(
        source,
        tokens,
        route_gates,
        expert_ids,
        owner_next[None, :],
        out_grad,
        expert_weights[0],
        first_moment[0],
        second_moment[0],
    )
    moe_out, tokens_grad, gate_grads, w_new, m_new, v_new = result
    return (moe_out, tokens_grad, gate_grads, w_new[None], m_new[None], v_new[None])


def solution(mesh):
    pairs = mesh.shape["expert"] // 2
    ys = 1
    while ys * ys * 4 <= pairs:
        ys *= 2
    by_token = P(("dp", "expert"), None)
    by_state = P("expert", "dp", None)
    return jax.shard_map(
        functools.partial(shards, (pairs // ys, ys)),
        mesh=mesh,
        in_specs=(by_token,) * 3 + (P(), P()) + (by_token,) + (by_state,) * 3,
        out_specs=(by_token,) * 3 + (by_state,) * 3,
        check_vma=False,
    )
```

time: 484 us -> 175 us (0.36); the launches traced: 477 us -> 173 us
  waiting for transfers between devices: 276 us -> 0 us
  Pallas kernels: 0 us -> 162 us
  local copies, waits for them, and re-layouts: 74.7 us -> 9.55 us
  starting transfers between devices: 49.7 us -> 0 us
  other arithmetic: 44.4 us -> 0.63 us
  matrix products: 17 us -> 0 us
  between operations: 14.7 us -> 0.67 us
    all_to_all x7 -> x0, waiting for transfers between devices: 276 us -> none  [the longest x1 199 us: shards(): lax.all_to_all(partial_value, 'dp', split_axis=0, concat_axis=0, tiled=True)]
    pallas_call x0 -> x1, Pallas kernels: none -> 162 us  [shards(): pl.pallas_call(functools.partial(kernel, (groups, experts, *grid)), out_s...]
    all_to_all x7 -> x0, starting transfers between devices: 49.6 us -> none  [the longest x1 12.9 us: shards(): lax.all_to_all(partial_value, 'dp', split_axis=0, concat_axis=0, tiled=True)]
    gather x7 -> x0, local copies, waits for them, and re-layouts: 21.8 us -> none  [the longest x2 8.26 us: shards(): returned_dx[destination].astype(jnp.float32)]
    reshape x9 -> x0, local copies, waits for them, and re-layouts: 17.2 us -> none  [the longest x1 3.62 us: shards(): routed.reshape(received.shape)]
    dot_general x6 -> x0, matrix products: 17 us -> none  [the longest x1 3.82 us: shards(): lax.dot_general(activation, weight_down, (((1,), (1,)), ((), ())), prefer...]
    all_to_all x3 -> x0, other arithmetic: 15.5 us -> none  [the longest x1 7.96 us: move_late(): lax.all_to_all(state_block.reshape(experts, -1), 'expert', split_axis=0,...]
    reduce_sum x8 -> x1, other arithmetic: 15 us -> 0.63 us  [shards(): source = jnp.sum(jnp.where(matches, owner_now[None, :], 0), axis=1)]
  transfers between devices with their start and end apart: 8 -> 0, of which waited for: 6 -> 0; matrix products, arithmetic and copies ran while one was open for 22% -> 0% of each run, Pallas kernels for 0% -> 0%
where the time goes in v1:
time: 175 us; the launch traced here: 173 us
  Pallas kernels  162 us (93%)
  local copies, waits for them, and re-layouts  9.55 us (5%)
    pallas_call x1, Pallas kernels, shards(): pl.pallas_call(functools.partial(kernel, (groups, experts, *grid)), out_s...  162 us
    unnamed x24, local copies, waits for them, and re-layouts  9.55 us

profile of v1, /device:TPU:1, one launch (start us, length us, event | category | flops | bytes accessed | tf_op | source)
XLA Modules:
  0.0 173.0 jit_solution(8585245480806473737)
XLA Ops:
  0.6 0.0 copy-start.6
  0.6 0.0 copy-start.7
  0.7 0.0 copy-start.4
  0.7 0.6 copy-done.6
  1.3 0.0 copy-done.7
  1.3 0.6 select_reduce_fusion.source
  1.9 0.0 copy-done.4
  1.9 0.7 copy.18.gates
  2.7 0.0 copy-done.5
  2.7 0.7 copy.19.ids
  3.4 162.1 %moe_step.1 = (bf16[128,2048]{1,0:T(8,128)(2,1)}, bf16[128,2048]{1,0:T(8,128)(2,1)}, f32[128,3]{1,0:T(8,128)}, bf16[128,1152]{1,0:T(8,128)(2,1)}, bf16[128,1152]{1,0:T(8,128)(2,1)}, /*index=5*/bf16[128,1152]{1,0:T(8,128)(2,1)}) custom-call(s32[32]{0:T(128)} %select_reduce_fusion.source, bf16[128,2048]{1,0:T(8,128)(2,1)} %tokens.1, f32[128,3]{1,0:T(8,128)} %copy.18.gates, ...), custom_call_target="tpu_custom_call" | custom-call | tf_op jit(solution)/shard_map/moe_step/pallas_call | solution.py:536
  165.6 1.5 copy.20
  167.0 0.0 copy-start
  167.1 1.9 %copy.26 = bf16[128,2048]{1,0:T(8,128)(2,1)} copy(bf16[128,2048]{1,0:T(8,128)(2,1)} %get-tuple-element.36) | data formatting | bytes 1048576
  169.0 0.0 copy-done
  169.0 0.0 copy-start.3
  169.0 0.8 copy.27
  169.8 0.3 copy-done.3
  170.1 0.0 copy-start.2
  170.1 0.7 copy.28
  170.8 0.4 copy-done.2
  171.2 0.7 copy.29
  171.9 0.4 copy-done.1
  172.3 0.7 copy.30
  (2 shorter events, 0.0 us)
Async XLA Ops:
  0.6 0.7 copy-start.6
  0.6 0.7 copy-start.7
  0.7 1.3 copy-start.4
  1.9 0.7 copy-start.5
  167.0 1.9 %copy-start = (bf16[128,2048]{1,0:T(8,128)(2,1)S(1)}, bf16[128,2048]{1,0:T(8,128)(2,1)}, u32[]{:S(2)}) copy-start(bf16[128,2048]{1,0:T(8,128)(2,1)} %get-tuple-element.37) | copy-start | bytes 1572868
  169.0 1.1 copy-start.3
  170.1 1.1 copy-start.2
  171.2 1.1 copy-start.1

commit v2 on v1

v2 whole, which is shorter than its diff:
```python
import functools

import jax
import jax.numpy as jnp
from jax import lax
from jax.experimental import pallas as pl
from jax.experimental.pallas import tpu as pltpu
from jax.sharding import PartitionSpec as P

MESH = pl.DeviceIdType.MESH
BF16 = jnp.bfloat16
F32 = jnp.float32

beta_one = 0.9
beta_two = 0.95
learn_rate = 0.003
adam_eps = 1e-08

SLOT = 16
WIDE, NARROW = 256, 128
X_STEPS, G_STEPS = 2, 4
CHUNKS = 2


def dot(a, b, dims):
    return lax.dot_general(a, b, (dims, ((), ())), preferred_element_type=F32)


def kernel(
    cfg,
    source,
    tokens,
    gates,
    ids,
    owner_next,
    out_grad,
    w_old,
    m_old,
    v_old,
    moe_out,
    tokens_grad,
    gate_grads,
    w_new,
    m_new,
    v_new,
    x_send,
    g_send,
    x_in,
    g_in,
    weights,
    gate_up,
    act,
    pre,
    ro_send,
    dx_send,
    ro_in,
    dx_in,
    sum_send,
    sum_in,
    part,
    place,
    place_t,
    high_t,
    low_t,
    gate_of,
    hop_w_a,
    hop_w_b,
    out_w_a,
    out_w_b,
    hop_m_a,
    hop_m_b,
    out_m_a,
    out_m_b,
    moments_old,
    moments,
    load_s,
    a2a_s,
    a2a_r,
    hop1_s,
    hop1_r,
    hop2_s,
    hop2_r,
    ag_s,
    ag_r,
    rs_s,
    rs_r,
):
    groups, experts, xs, ys = cfg
    hop_a, hop_b = (hop_w_a, hop_m_a), (hop_w_b, hop_m_b)
    out_a, out_b = (out_w_a, out_m_a), (out_w_b, out_m_b)
    dp = lax.axis_index("dp")
    me = lax.axis_index("expert")
    tok, width = tokens.shape
    rows, cols = w_old.shape
    hid = cols // 3
    slots = experts * SLOT
    others = experts - 1
    n_wide = cols // WIDE
    n_row = rows // SLOT
    half = groups // 2
    part_rows = rows // CHUNKS
    right = lax.rem(dp + 1, groups)
    left = lax.rem(dp + groups - 1, groups)
    y_bits = ys.bit_length()
    low_bits = (1 << y_bits) - 1

    def peer(i):
        off = (i * 11) & (experts - 1)
        x_part = ((me >> y_bits) + (off >> y_bits)) & (xs - 1)
        y_part = ((me & low_bits & ~1) + (off & low_bits & ~1)) & low_bits
        return (x_part << y_bits) | y_part | ((me ^ off) & 1)

    def each_peer(low, high, body):
        def step(i, carry):
            body(peer(i))
            return carry

        lax.fori_loop(low, high, step, 0)

    def remote(src, dst, ssem, rsem, device):
        pltpu.make_async_remote_copy(
            src_ref=src,
            dst_ref=dst,
            send_sem=ssem,
            recv_sem=rsem,
            device_id=device,
            device_id_type=MESH,
        ).start()

    def await_bytes(ref, sem):
        pltpu.make_async_copy(ref, ref, sem).wait()

    loads = [
        pltpu.make_async_copy(ref, moments_old.at[n], load_s.at[n])
        for n, ref in enumerate((m_old, v_old))
    ]
    for load in loads:
        load.start()

    barrier = pltpu.get_barrier_semaphore()
    each_peer(
        1,
        experts,
        lambda d: pl.semaphore_signal(
            barrier, inc=1, device_id=(dp, d), device_id_type=MESH
        ),
    )
    for z in (left, right):
        pl.semaphore_signal(barrier, inc=1, device_id=(z, me), device_id_type=MESH)
    pl.semaphore_wait(barrier, experts + 1)

    shift = n_wide.bit_length() - 1

    def piece(ref, lead, relay, base=0):
        return ref.at[
            (
                *lead,
                pl.ds(pl.multiple_of(base + (relay >> shift) * SLOT, SLOT), SLOT),
                pl.ds(pl.multiple_of((relay & (n_wide - 1)) * WIDE, WIDE), WIDE),
            )
        ]

    def rest(ref, lead, relay, base=0):
        return ref.at[
            (
                *lead,
                pl.ds(pl.multiple_of(base + (relay >> shift) * SLOT, SLOT), SLOT),
                pl.ds(n_wide * WIDE, NARROW),
            )
        ]

    def narrow(a, device):
        return (device & (n_wide - 1)) == a % n_wide

    leads = ((), (slice(None),))

    def hop_one(a, ref):
        def one(d):
            remote(
                piece(ref, leads[a], d), hop_a[a].at[me], hop1_s.at[a, 0], hop1_r.at[a, 0], (dp, d)
            )

            @pl.when(narrow(a, d))
            def _():
                remote(
                    rest(ref, leads[a], d), hop_b[a].at[me], hop1_s.at[a, 1], hop1_r.at[a, 1], (dp, d)
                )

        each_peer(1, experts, one)
        hop_a[a][me] = piece(ref, leads[a], me)[...]

        @pl.when(narrow(a, me))
        def _():
            hop_b[a][me] = rest(ref, leads[a], me)[...]

    def hop_two(a, ref, base):
        def pass_on(n, hop, out, part_of):
            await_bytes(hop.at[pl.ds(0, others)], hop1_r.at[a, n])

            def pick(s, carry):
                out[s] = hop[source[s]]
                return carry

            lax.fori_loop(0, experts, pick, 0)
            each_peer(
                1,
                experts,
                lambda d: remote(
                    out.at[d],
                    part_of(ref, leads[a], me, base),
                    hop2_s.at[a, n],
                    hop2_r.at[a, n],
                    (dp, d),
                ),
            )
            part_of(ref, leads[a], me, base)[...] = out[me]

        pass_on(0, hop_a[a], out_a[a], piece)

        @pl.when(narrow(a, me))
        def _():
            pass_on(1, hop_b[a], out_b[a], rest)

    def narrow_wait(a, sem):
        @pl.when(narrow(a, me))
        def _():
            await_bytes(hop_b[a].at[pl.ds(0, n_row - 1)], sem)

        @pl.when(jnp.logical_not(narrow(a, me)))
        def _():
            await_bytes(hop_b[a].at[pl.ds(0, n_row)], sem)

    def arrived(a):
        await_bytes(hop_a[a].at[pl.ds(0, others)], hop2_r.at[a, 0])
        narrow_wait(a, hop2_r.at[a, 1])

    def hops_sent(a):
        await_bytes(hop_a[a].at[pl.ds(0, others)], hop1_s.at[a, 0])
        narrow_wait(a, hop1_s.at[a, 1])
        await_bytes(hop_a[a].at[pl.ds(0, others)], hop2_s.at[a, 0])

        @pl.when(narrow(a, me))
        def _():
            await_bytes(hop_b[a].at[pl.ds(0, others)], hop2_s.at[a, 1])

    def zone(z, ch=0, size=None):
        start = ((z + groups) & (groups - 1)) * rows + ch * part_rows
        return pl.ds(pl.multiple_of(start, part_rows), size or rows)

    def on_far(way, ch):
        return (ch < CHUNKS // 2) == (way == 0)

    hop_one(0, w_old)

    expert_row = lax.broadcasted_iota(jnp.int32, (experts, tok), 0)
    hits = [(ids[r : r + 1, :] == expert_row).astype(F32) for r in range(3)]
    before = lax.broadcasted_iota(jnp.int32, (tok, tok), 0) < lax.broadcasted_iota(
        jnp.int32, (tok, tok), 1
    )
    position = dot(
        (hits[0] + hits[1] + hits[2]).astype(BF16),
        before.astype(F32).astype(BF16),
        ((1,), (0,)),
    )
    diagonal = lax.broadcasted_iota(jnp.int32, (experts, experts), 0) == lax.broadcasted_iota(
        jnp.int32, (experts, experts), 1
    )
    holder = jnp.sum(
        jnp.where(diagonal, owner_next[...].astype(F32), 0.0), axis=1, keepdims=True
    )
    row_at = holder * SLOT + position
    target = [
        jnp.sum(h * row_at, axis=0, keepdims=True).astype(jnp.int32) for h in hits
    ]
    slot_row = lax.broadcasted_iota(jnp.int32, (slots, tok), 0)
    spread = jnp.zeros((slots, tok), F32)
    weighted = jnp.zeros((slots, tok), F32)
    for r in range(3):
        here = slot_row == target[r]
        spread = spread + here.astype(F32)
        weighted = weighted + jnp.where(here, gates[r : r + 1, :], 0.0)
    place[...] = spread.astype(BF16)
    block = min(256, width)

    def gather_x(c, carry):
        at = pl.ds(pl.multiple_of(c * block, block), block)
        x_send[:, at] = dot(place[...], tokens[:, at], ((1,), (0,))).astype(BF16)
        return carry

    lax.fori_loop(0, width // block, gather_x, 0)

    hop_two(0, weights, dp * rows)

    mine = pl.ds(pl.multiple_of(me * SLOT, SLOT), SLOT)

    def send_rows(n, src, dst, low, high):
        each_peer(
            low,
            high,
            lambda d: remote(
                src.at[pl.ds(pl.multiple_of(d * SLOT, SLOT), SLOT)],
                dst.at[mine],
                a2a_s.at[n],
                a2a_r.at[n],
                (dp, d),
            ),
        )

    def rows_arrived(n, ref):
        await_bytes(ref.at[pl.ds(0, others * SLOT)], a2a_r.at[n])

    def share(steps, k):
        per = -(-others // steps)
        return 1 + jnp.minimum(k * per, others), 1 + jnp.minimum((k + 1) * per, others)

    send_rows(0, x_send, x_in, *share(X_STEPS, 0))
    x_in[mine, :] = x_send[mine, :]

    def gather_copy(way, k, ch):
        at = zone(dp - k if way == 0 else dp + k, ch, part_rows)
        remote(
            weights.at[at],
            weights.at[at],
            ag_s.at[way, k, ch],
            ag_r.at[way, k, ch],
            (right if way == 0 else left, me),
        )

    def gathered(way, k, ch):
        z = dp - k - 1 if way == 0 else dp + k + 1
        await_bytes(weights.at[zone(z, ch, part_rows)], ag_r.at[way, k, ch])

    arrived(0)
    for ch in range(CHUNKS):
        for way in (0, 1):
            gather_copy(way, 0, ch)

    for k in range(1, X_STEPS):
        send_rows(0, x_send, x_in, *share(X_STEPS, k))

    gate_of[...] = jnp.sum(weighted, axis=1, keepdims=True)

    def gather_g(c, carry):
        at = pl.ds(pl.multiple_of(c * block, block), block)
        g_send[:, at] = (
            dot(place[...], out_grad[:, at], ((1,), (0,))) * gate_of[...]
        ).astype(BF16)
        return carry

    lax.fori_loop(0, width // block, gather_g, 0)
    g_in[mine, :] = g_send[mine, :]

    def gather_step(k, carry):
        for ch in range(CHUNKS):
            for way in (0, 1):
                gathered(way, k, ch)

                if on_far(way, ch):
                    gather_copy(way, k + 1, ch)
                else:

                    @pl.when(k + 1 < half - 1)
                    def _():
                        gather_copy(way, k + 1, ch)

        @pl.when(k < G_STEPS)
        def _():
            send_rows(1, g_send, g_in, *share(G_STEPS, k))

        return carry

    lax.fori_loop(0, half - 1, gather_step, 0)
    for k in range(half - 1, G_STEPS):
        send_rows(1, g_send, g_in, *share(G_STEPS, k))

    for load in loads:
        load.wait()
    hop_one(1, moments_old)

    weighted_t = weighted.T
    high = weighted_t.astype(BF16)
    high_t[...] = high
    low_t[...] = (weighted_t - high.astype(F32)).astype(BF16)
    place_t[...] = spread.T.astype(BF16)

    def hidden_sums(rows_here, base, zs, first):
        step = min(256, hid) if base == 0 else hid
        for c in range(base, 2 * hid if base == 0 else 3 * hid, step):
            total = None
            for z in zs:
                term = dot(
                    jnp.concatenate([rows_here[:, zone(i)] for i in z], axis=1),
                    jnp.concatenate([weights[zone(i), c : c + step] for i in z], axis=0),
                    ((1,), (0,)),
                )
                total = term if total is None else total + term
            gate_up[:, c : c + step] = total if first else gate_up[:, c : c + step] + total

    near = [dp + half + 1 + n for n in range(groups - 1)]
    near = [near[n : n + 2] for n in range(0, groups - 1, 2)]
    rows_arrived(0, x_in)
    hidden_sums(x_in, 0, near, True)
    rows_arrived(1, g_in)
    hidden_sums(g_in, 2 * hid, near, True)
    for ch in range(CHUNKS):
        gathered(0 if on_far(0, ch) else 1, half - 1, ch)
    hidden_sums(x_in, 0, [[dp + half]], False)
    hidden_sums(g_in, 2 * hid, [[dp + half]], False)

    height = min(64, slots)

    def hidden(c, carry):
        at = pl.ds(pl.multiple_of(c * height, height), height)
        gate = gate_up[at, 0:hid]
        up = gate_up[at, hid : 2 * hid]
        grad = gate_up[at, 2 * hid : 3 * hid]
        sig = jax.nn.sigmoid(gate)
        act[at, :] = (gate * sig * up).astype(BF16)
        pre[at, 0:hid] = (grad * up * sig * (1.0 + gate * (1.0 - sig))).astype(BF16)
        pre[at, hid : 2 * hid] = (grad * (gate * sig)).astype(BF16)
        return carry

    lax.fori_loop(0, slots // height, hidden, 0)

    def partial(z, n):
        at = zone(z)
        part[n, :, 0 : 2 * hid] = dot(x_in[:, at], pre[...], ((0,), (0,)))
        part[n, :, 2 * hid : 3 * hid] = dot(g_in[:, at], act[...], ((0,), (0,)))

    def sum_copy(way, k, ch):
        at = pl.ds(ch * part_rows, part_rows)
        remote(
            sum_send.at[way, k, at],
            sum_in.at[way, k, at],
            rs_s.at[way, k, ch],
            rs_r.at[way, k, ch],
            (right if way == 0 else left, me),
        )

    def sum_arrived(way, k, ch):
        at = pl.ds(ch * part_rows, part_rows)
        await_bytes(sum_in.at[way, k, at], rs_r.at[way, k, ch])

    partial(dp + half, 0)
    for ch in range(CHUNKS):
        way = 0 if on_far(0, ch) else 1
        at = pl.ds(ch * part_rows, part_rows)
        sum_send[way, 0, at] = part[0, at].astype(BF16)
        sum_copy(way, 0, ch)

    def route_out(c, carry):
        at = pl.ds(pl.multiple_of(c * block, block), block)
        ro_send[:, at] = dot(act[...], weights[at, 2 * hid : 3 * hid], ((1,), (1,))).astype(BF16)
        return carry

    lax.fori_loop(0, width // block, route_out, 0)
    send_rows(2, ro_send, ro_in, 1, experts)
    ro_in[mine, :] = ro_send[mine, :]

    def sum_step(k, carry):
        partial(dp + half - k, 0)
        partial(dp - half + k, 1)

        for ch in range(CHUNKS):
            at = pl.ds(ch * part_rows, part_rows)
            for way in (0, 1):

                def add():
                    sum_arrived(way, k - 1, ch)
                    sum_send[way, k, at] = (
                        part[way, at] + sum_in[way, k - 1, at].astype(F32)
                    ).astype(BF16)

                if on_far(way, ch):
                    add()
                else:
                    pl.when(k > 1)(add)

                    @pl.when(k == 1)
                    def _():
                        sum_send[way, k, at] = part[way, at].astype(BF16)

                sum_copy(way, k, ch)
        return carry

    def give_dx():
        def dx_out(c, carry):
            at = pl.ds(pl.multiple_of(c * block, block), block)
            dx_send[:, at] = dot(pre[...], weights[at, 0 : 2 * hid], ((1,), (1,))).astype(BF16)
            return carry

        lax.fori_loop(0, width // block, dx_out, 0)
        send_rows(3, dx_send, dx_in, 1, experts)
        dx_in[mine, :] = dx_send[mine, :]
        hop_two(1, moments, 0)

    lax.fori_loop(1, 2, sum_step, 0)
    give_dx()
    lax.fori_loop(2, half, sum_step, 0)
    partial(dp, 0)

    rows_arrived(2, ro_in)

    def combine(c, total):
        at = pl.ds(pl.multiple_of(c * block, block), block)
        rows_here = ro_in[:, at]
        moe_out[:, at] = (
            dot(high_t[...], rows_here, ((1,), (0,))) + dot(low_t[...], rows_here, ((1,), (0,)))
        ).astype(BF16)
        return total + dot(rows_here, out_grad[:, at], ((1,), (1,)))

    products = lax.fori_loop(0, width // block, combine, jnp.zeros((slots, tok), F32))
    for r in range(3):
        gate_grads[r : r + 1, :] = jnp.sum(
            jnp.where(slot_row == target[r], products, 0.0), axis=0, keepdims=True
        )
    rows_arrived(3, dx_in)

    def combine_dx(c, carry):
        at = pl.ds(pl.multiple_of(c * block, block), block)
        tokens_grad[:, at] = dot(place_t[...], dx_in[:, at], ((1,), (0,))).astype(BF16)
        return carry

    lax.fori_loop(0, width // block, combine_dx, 0)

    arrived(1)
    for ch in range(CHUNKS):
        for way in (0, 1):
            sum_arrived(way, half - 1, ch)
    w_base = dp * rows

    def adam(c, carry):
        at = pl.ds(pl.multiple_of(c * SLOT, SLOT), SLOT)
        grad = (
            part[0, at]
            + sum_in[0, half - 1, at].astype(F32)
            + sum_in[1, half - 1, at].astype(F32)
        )
        first = beta_one * moments[0, at].astype(F32) + (1.0 - beta_one) * grad
        second = beta_two * moments[1, at].astype(F32) + (1.0 - beta_two) * grad * grad
        old = weights[pl.ds(pl.multiple_of(w_base + c * SLOT, SLOT), SLOT), :].astype(F32)
        w_new[at, :] = (old - learn_rate * first / (jnp.sqrt(second) + adam_eps)).astype(BF16)
        m_new[at, :] = first.astype(BF16)
        v_new[at, :] = second.astype(BF16)
        return carry

    lax.fori_loop(0, rows // SLOT, adam, 0)

    for n, ref in enumerate((x_send, g_send, ro_send, dx_send)):
        await_bytes(ref.at[pl.ds(0, others * SLOT)], a2a_s.at[n])
    for a in range(2):
        hops_sent(a)
    for ch in range(CHUNKS):
        at = pl.ds(ch * part_rows, part_rows)
        for way in (0, 1):

            def left_here(k, carry):
                await_bytes(sum_send.at[way, k, at], ag_s.at[way, k, ch])
                await_bytes(sum_send.at[way, k + 1, at], rs_s.at[way, k + 1, ch])
                return carry

            lax.fori_loop(0, half - 1, left_here, 0)
        way = 0 if on_far(0, ch) else 1
        await_bytes(sum_send.at[way, half - 1, at], ag_s.at[way, half - 1, ch])
        await_bytes(sum_send.at[way, 0, at], rs_s.at[way, 0, ch])


def shards(
    grid,
    tokens,
    route_gates,
    expert_ids,
    owner_now,
    owner_next,
    out_grad,
    expert_weights,
    first_moment,
    second_moment,
):
    groups, experts = lax.axis_size("dp"), lax.axis_size("expert")
    tok, width = tokens.shape
    _, rows, cols = expert_weights.shape
    hid = cols // 3
    slots = experts * SLOT
    half = groups // 2
    matches = owner_next[None, :] == jnp.arange(experts, dtype=jnp.int32)[:, None]
    source = jnp.sum(jnp.where(matches, owner_now[None, :], 0), axis=1)
    vmem = pl.BlockSpec(memory_space=pltpu.VMEM)
    dma = pltpu.SemaphoreType.DMA
    state = jax.ShapeDtypeStruct((rows, cols), BF16)
    result = pl.pallas_call(
        functools.partial(kernel, (groups, experts, *grid)),
        out_shape=(
            jax.ShapeDtypeStruct((tok, width), BF16),
            jax.ShapeDtypeStruct((tok, width), BF16),
            jax.ShapeDtypeStruct(route_gates.shape[::-1], F32),
            state,
            state,
            state,
        ),
        in_specs=[pl.BlockSpec(memory_space=pltpu.SMEM)]
        + [vmem] * 6
        + [pl.BlockSpec(memory_space=pl.ANY)] * 2,
        out_specs=(vmem,) * 6,
        scratch_shapes=[
            pltpu.VMEM((slots, width), BF16),
            pltpu.VMEM((slots, width), BF16),
            pltpu.VMEM((slots, width), BF16),
            pltpu.VMEM((slots, width), BF16),
            pltpu.VMEM((width, cols), BF16),
            pltpu.VMEM((slots, cols), F32),
            pltpu.VMEM((slots, hid), BF16),
            pltpu.VMEM((slots, 2 * hid), BF16),
            pltpu.VMEM((slots, width), BF16),
            pltpu.VMEM((slots, width), BF16),
            pltpu.VMEM((slots, width), BF16),
            pltpu.VMEM((slots, width), BF16),
            pltpu.VMEM((2, half, rows, cols), BF16),
            pltpu.VMEM((2, half, rows, cols), BF16),
            pltpu.VMEM((2, rows, cols), F32),
            pltpu.VMEM((slots, tok), BF16),
            pltpu.VMEM((tok, slots), BF16),
            pltpu.VMEM((tok, slots), BF16),
            pltpu.VMEM((tok, slots), BF16),
            pltpu.VMEM((slots, 1), F32),
            pltpu.VMEM((experts, SLOT, WIDE), BF16),
            pltpu.VMEM((experts, SLOT, NARROW), BF16),
            pltpu.VMEM((experts, SLOT, WIDE), BF16),
            pltpu.VMEM((experts, SLOT, NARROW), BF16),
            pltpu.VMEM((experts, 2, SLOT, WIDE), BF16),
            pltpu.VMEM((experts, 2, SLOT, NARROW), BF16),
            pltpu.VMEM((experts, 2, SLOT, WIDE), BF16),
            pltpu.VMEM((experts, 2, SLOT, NARROW), BF16),
            pltpu.VMEM((2, rows, cols), BF16),
            pltpu.VMEM((2, rows, cols), BF16),
            dma((2,)),
            dma((4,)),
            dma((4,)),
            dma((2, 2)),
            dma((2, 2)),
            dma((2, 2)),
            dma((2, 2)),
            dma((2, half, CHUNKS)),
            dma((2, half, CHUNKS)),
            dma((2, half, CHUNKS)),
            dma((2, half, CHUNKS)),
        ],
        compiler_params=pltpu.CompilerParams(
            collective_id=0, has_side_effects=True, vmem_limit_bytes=60 * 2**20
        ),
        name="moe_step",
    )(
        source,
        tokens,
        route_gates.T,
        expert_ids.T,
        owner_next[None, :],
        out_grad,
        expert_weights[0],
        first_moment[0],
        second_moment[0],
    )
    moe_out, tokens_grad, gate_grads, w_new, m_new, v_new = result
    return (moe_out, tokens_grad, gate_grads.T, w_new[None], m_new[None], v_new[None])


def solution(mesh):
    pairs = mesh.shape["expert"] // 2
    ys = 1
    while ys * ys * 4 <= pairs:
        ys *= 2
    by_token = P(("dp", "expert"), None)
    by_state = P("expert", "dp", None)
    return jax.shard_map(
        functools.partial(shards, (pairs // ys, ys)),
        mesh=mesh,
        in_specs=(by_token,) * 3 + (P(), P()) + (by_token,) + (by_state,) * 3,
        out_specs=(by_token,) * 3 + (by_state,) * 3,
        check_vma=False,
    )
```

time: 175 us -> 161 us (0.920); the launches traced: 173 us -> 161 us
  Pallas kernels: 162 us -> 153 us
  local copies, waits for them, and re-layouts: 9.55 us -> 6.83 us
    pallas_call x1, Pallas kernels: 162 us -> 153 us  [shards(): pl.pallas_call(functools.partial(kernel, (groups, experts, *grid)), out_s...]
    unnamed x24 -> x20, local copies, waits for them, and re-layouts: 9.55 us -> 6.83 us
where the time goes in v2:
time: 161 us
  Pallas kernels  153 us (95%)
  local copies, waits for them, and re-layouts  6.83 us (4%)
    pallas_call x1, Pallas kernels, shards(): pl.pallas_call(functools.partial(kernel, (groups, experts, *grid)), out_s...  153 us
    unnamed x20, local copies, waits for them, and re-layouts  6.83 us

profile of v2, /device:TPU:1, one launch (start us, length us, event | category | flops | bytes accessed | tf_op | source)
XLA Modules:
  0.0 161.1 jit_solution(119359924219987555)
XLA Ops:
  0.6 0.0 copy-start.5
  0.6 0.0 copy-start.6
  0.7 0.6 copy-done.5
  1.3 0.0 copy-done.6
  1.3 0.6 select_reduce_fusion.source
  1.9 153.0 %moe_step.1 = (bf16[128,2048]{1,0:T(8,128)(2,1)}, bf16[128,2048]{1,0:T(8,128)(2,1)}, f32[3,128]{1,0:T(4,128)}, bf16[128,1152]{1,0:T(8,128)(2,1)}, bf16[128,1152]{1,0:T(8,128)(2,1)}, /*index=5*/bf16[128,1152]{1,0:T(8,128)(2,1)}) custom-call(s32[32]{0:T(128)} %select_reduce_fusion.source, bf16[128,2048]{1,0:T(8,128)(2,1)} %tokens.1, f32[3,128]{1,0:T(4,128)} %bitcast.16, ...), custom_call_target="tpu_custom_call" | custom-call | tf_op jit(solution)/shard_map/moe_step/pallas_call | solution.py:591
  154.9 0.0 copy-start
  154.9 1.9 %copy.21 = bf16[128,2048]{1,0:T(8,128)(2,1)} copy(bf16[128,2048]{1,0:T(8,128)(2,1)} %get-tuple-element.24) | data formatting | bytes 1048576
  156.9 0.0 copy-done
  156.9 0.0 copy-start.4
  156.9 0.0 copy-start.3
  156.9 0.8 copy.22
  157.7 0.0 copy-done.4
  157.7 0.6 copy.23
  158.2 0.0 copy-done.3
  158.2 0.0 copy-start.2
  158.3 0.7 copy.24
  159.0 0.4 copy-done.2
  159.3 0.0 copy-start.1
  159.3 0.7 copy.25
  160.0 0.4 copy-done.1
  160.4 0.7 copy.26
Async XLA Ops:
  0.6 0.7 copy-start.5
  0.6 0.7 copy-start.6
  154.9 2.0 %copy-start = (bf16[128,2048]{1,0:T(8,128)(2,1)S(1)}, bf16[128,2048]{1,0:T(8,128)(2,1)}, u32[]{:S(2)}) copy-start(bf16[128,2048]{1,0:T(8,128)(2,1)} %get-tuple-element.25) | copy-start | bytes 1572868
  156.9 0.8 copy-start.4
  156.9 1.4 copy-start.3
  158.2 1.1 copy-start.2
  159.3 1.1 copy-start.1

commit v3 on v2

--- a/solution.py
+++ b/solution.py
@@ -67,10 +67,10 @@
     hop_w_b,
     out_w_a,
     out_w_b,
-    hop_m_a,
-    hop_m_b,
-    out_m_a,
-    out_m_b,
+    hop_m,
+    hop_v,
+    out_m,
+    out_v,
     moments_old,
     moments,
     load_s,
@@ -86,8 +86,8 @@
     rs_r,
 ):
     groups, experts, xs, ys = cfg
-    hop_a, hop_b = (hop_w_a, hop_m_a), (hop_w_b, hop_m_b)
-    out_a, out_b = (out_w_a, out_m_a), (out_w_b, out_m_b)
+    hop_a, hop_b, out_a, out_b = (hop_w_a,), (hop_w_b,), (out_w_a,), (out_w_b,)
+    hops, outs = (None, hop_m, hop_v), (None, out_m, out_v)
     dp = lax.axis_index("dp")
     me = lax.axis_index("expert")
     tok, width = tokens.shape
@@ -172,7 +172,7 @@
     def narrow(a, device):
         return (device & (n_wide - 1)) == a % n_wide
 
-    leads = ((), (slice(None),))
+    leads = ((),)
 
     def hop_one(a, ref):
         def one(d):
@@ -242,6 +242,69 @@
         @pl.when(narrow(a, me))
         def _():
             await_bytes(hop_b[a].at[pl.ds(0, others)], hop2_s.at[a, 1])
+
+    def relay(a, p):
+        if n_row * 4 != experts:
+            return p
+        x = p // 2
+        return (x * ys + 2 * (p % 2) + (x + a) % 2) * 2 + a // 2
+
+    relays = [[relay(a, p) for p in range(n_row)] for a in range(3)]
+    my_piece = [sum(jnp.where(me == d, p, 0) for p, d in enumerate(ds)) for ds in relays]
+    is_relay = [sum(jnp.where(me == d, 1, 0) for d in ds) > 0 for ds in relays]
+
+    def rows_at(ref, p, base=0):
+        return ref.at[pl.ds(pl.multiple_of(base + p * SLOT, SLOT), SLOT)]
+
+    def moment_hop_one(a, ref):
+        for p, d in enumerate(relays[a]):
+
+            @pl.when(me != d)
+            def _():
+                remote(rows_at(ref, p), hops[a].at[me], hop1_s.at[a, 0], hop1_r.at[a, 0], (dp, d))
+
+            @pl.when(me == d)
+            def _():
+                hops[a][me] = rows_at(ref, p)[...]
+
+    def moment_hop_two(a, ref, base):
+        hop, out = hops[a], outs[a]
+
+        @pl.when(is_relay[a])
+        def _():
+            await_bytes(hop.at[pl.ds(0, others)], hop1_r.at[a, 0])
+
+            def pick(s, carry):
+                out[s] = hop[source[s]]
+                return carry
+
+            lax.fori_loop(0, experts, pick, 0)
+            goal = rows_at(ref, my_piece[a], base)
+            each_peer(
+                1,
+                experts,
+                lambda d: remote(out.at[d], goal, hop2_s.at[a, 0], hop2_r.at[a, 0], (dp, d)),
+            )
+            goal[...] = out[me]
+
+    def pieces_wait(a, sem):
+        @pl.when(is_relay[a])
+        def _():
+            await_bytes(hops[a].at[pl.ds(0, n_row - 1)], sem)
+
+        @pl.when(jnp.logical_not(is_relay[a]))
+        def _():
+            await_bytes(hops[a].at[pl.ds(0, n_row)], sem)
+
+    def moment_arrived(a):
+        pieces_wait(a, hop2_r.at[a, 0])
+
+    def moment_hops_sent(a):
+        pieces_wait(a, hop1_s.at[a, 0])
+
+        @pl.when(is_relay[a])
+        def _():
+            await_bytes(outs[a].at[pl.ds(0, others)], hop2_s.at[a, 0])
 
     def zone(z, ch=0, size=None):
         start = ((z + groups) & (groups - 1)) * rows + ch * part_rows
@@ -316,6 +379,18 @@
     send_rows(0, x_send, x_in, *share(X_STEPS, 0))
     x_in[mine, :] = x_send[mine, :]
 
+    gate_of[...] = jnp.sum(weighted, axis=1, keepdims=True)
+
+    def gather_g(c, carry):
+        at = pl.ds(pl.multiple_of(c * block, block), block)
+        g_send[:, at] = (
+            dot(place[...], out_grad[:, at], ((1,), (0,))) * gate_of[...]
+        ).astype(BF16)
+        return carry
+
+    lax.fori_loop(0, width // block, gather_g, 0)
+    g_in[mine, :] = g_send[mine, :]
+
     def gather_copy(way, k, ch):
         at = zone(dp - k if way == 0 else dp + k, ch, part_rows)
         remote(
@@ -338,18 +413,6 @@
     for k in range(1, X_STEPS):
         send_rows(0, x_send, x_in, *share(X_STEPS, k))
 
-    gate_of[...] = jnp.sum(weighted, axis=1, keepdims=True)
-
-    def gather_g(c, carry):
-        at = pl.ds(pl.multiple_of(c * block, block), block)
-        g_send[:, at] = (
-            dot(place[...], out_grad[:, at], ((1,), (0,))) * gate_of[...]
-        ).astype(BF16)
-        return carry
-
-    lax.fori_loop(0, width // block, gather_g, 0)
-    g_in[mine, :] = g_send[mine, :]
-
     def gather_step(k, carry):
         for ch in range(CHUNKS):
             for way in (0, 1):
@@ -375,7 +438,8 @@
 
     for load in loads:
         load.wait()
-    hop_one(1, moments_old)
+    moment_hop_one(1, moments_old.at[0])
+    moment_hop_one(2, moments_old.at[1])
 
     weighted_t = weighted.T
     high = weighted_t.astype(BF16)
@@ -402,30 +466,54 @@
     hidden_sums(x_in, 0, near, True)
     rows_arrived(1, g_in)
     hidden_sums(g_in, 2 * hid, near, True)
+    moment_hop_two(1, moments.at[0], 0)
+    moment_hop_two(2, moments.at[1], 0)
     for ch in range(CHUNKS):
         gathered(0 if on_far(0, ch) else 1, half - 1, ch)
     hidden_sums(x_in, 0, [[dp + half]], False)
+
+    height = min(64, slots)
+
+    def each_part(body):
+        def step(c, carry):
+            body(pl.ds(pl.multiple_of(c * height, height), height))
+            return carry
+
+        lax.fori_loop(0, slots // height, step, 0)
+
+    def forward(at):
+        gate = gate_up[at, 0:hid]
+        act[at, :] = (gate * jax.nn.sigmoid(gate) * gate_up[at, hid : 2 * hid]).astype(BF16)
+
+    each_part(forward)
+
+    def route_out(c, carry):
+        at = pl.ds(pl.multiple_of(c * block, block), block)
+        ro_send[:, at] = dot(act[...], weights[at, 2 * hid : 3 * hid], ((1,), (1,))).astype(BF16)
+        return carry
+
+    lax.fori_loop(0, width // block, route_out, 0)
+    send_rows(2, ro_send, ro_in, 1, experts)
+    ro_in[mine, :] = ro_send[mine, :]
+
     hidden_sums(g_in, 2 * hid, [[dp + half]], False)
 
-    height = min(64, slots)
-
-    def hidden(c, carry):
-        at = pl.ds(pl.multiple_of(c * height, height), height)
+    def backward(at):
         gate = gate_up[at, 0:hid]
         up = gate_up[at, hid : 2 * hid]
         grad = gate_up[at, 2 * hid : 3 * hid]
         sig = jax.nn.sigmoid(gate)
-        act[at, :] = (gate * sig * up).astype(BF16)
         pre[at, 0:hid] = (grad * up * sig * (1.0 + gate * (1.0 - sig))).astype(BF16)
         pre[at, hid : 2 * hid] = (grad * (gate * sig)).astype(BF16)
-        return carry
-
-    lax.fori_loop(0, slots // height, hidden, 0)
-
-    def partial(z, n):
-        at = zone(z)
-        part[n, :, 0 : 2 * hid] = dot(x_in[:, at], pre[...], ((0,), (0,)))
-        part[n, :, 2 * hid : 3 * hid] = dot(g_in[:, at], act[...], ((0,), (0,)))
+
+    each_part(backward)
+
+    def partial(*zs):
+        x_side = jnp.concatenate([x_in[:, zone(z)] for z in zs], axis=1)
+        g_side = jnp.concatenate([g_in[:, zone(z)] for z in zs], axis=1)
+        high = len(zs) * rows
+        part[0:high, 0 : 2 * hid] = dot(x_side, pre[...], ((0,), (0,)))
+        part[0:high, 2 * hid : 3 * hid] = dot(g_side, act[...], ((0,), (0,)))
 
     def sum_copy(way, k, ch):
         at = pl.ds(ch * part_rows, part_rows)
@@ -441,34 +529,25 @@
         at = pl.ds(ch * part_rows, part_rows)
         await_bytes(sum_in.at[way, k, at], rs_r.at[way, k, ch])
 
-    partial(dp + half, 0)
+    partial(dp + half)
     for ch in range(CHUNKS):
         way = 0 if on_far(0, ch) else 1
         at = pl.ds(ch * part_rows, part_rows)
-        sum_send[way, 0, at] = part[0, at].astype(BF16)
+        sum_send[way, 0, at] = part[at, :].astype(BF16)
         sum_copy(way, 0, ch)
 
-    def route_out(c, carry):
-        at = pl.ds(pl.multiple_of(c * block, block), block)
-        ro_send[:, at] = dot(act[...], weights[at, 2 * hid : 3 * hid], ((1,), (1,))).astype(BF16)
-        return carry
-
-    lax.fori_loop(0, width // block, route_out, 0)
-    send_rows(2, ro_send, ro_in, 1, experts)
-    ro_in[mine, :] = ro_send[mine, :]
-
     def sum_step(k, carry):
-        partial(dp + half - k, 0)
-        partial(dp - half + k, 1)
+        partial(dp + half - k, dp - half + k)
 
         for ch in range(CHUNKS):
             at = pl.ds(ch * part_rows, part_rows)
             for way in (0, 1):
+                own = pl.ds(way * rows + ch * part_rows, part_rows)
 
                 def add():
                     sum_arrived(way, k - 1, ch)
                     sum_send[way, k, at] = (
-                        part[way, at] + sum_in[way, k - 1, at].astype(F32)
+                        part[own, :] + sum_in[way, k - 1, at].astype(F32)
                     ).astype(BF16)
 
                 if on_far(way, ch):
@@ -478,7 +557,7 @@
 
                     @pl.when(k == 1)
                     def _():
-                        sum_send[way, k, at] = part[way, at].astype(BF16)
+                        sum_send[way, k, at] = part[own, :].astype(BF16)
 
                 sum_copy(way, k, ch)
         return carry
@@ -492,12 +571,11 @@
         lax.fori_loop(0, width // block, dx_out, 0)
         send_rows(3, dx_send, dx_in, 1, experts)
         dx_in[mine, :] = dx_send[mine, :]
-        hop_two(1, moments, 0)
 
     lax.fori_loop(1, 2, sum_step, 0)
     give_dx()
     lax.fori_loop(2, half, sum_step, 0)
-    partial(dp, 0)
+    partial(dp)
 
     rows_arrived(2, ro_in)
 
@@ -514,16 +592,8 @@
         gate_grads[r : r + 1, :] = jnp.sum(
             jnp.where(slot_row == target[r], products, 0.0), axis=0, keepdims=True
         )
-    rows_arrived(3, dx_in)
-
-    def combine_dx(c, carry):
-        at = pl.ds(pl.multiple_of(c * block, block), block)
-        tokens_grad[:, at] = dot(place_t[...], dx_in[:, at], ((1,), (0,))).astype(BF16)
-        return carry
-
-    lax.fori_loop(0, width // block, combine_dx, 0)
-
-    arrived(1)
+    moment_arrived(1)
+    moment_arrived(2)
     for ch in range(CHUNKS):
         for way in (0, 1):
             sum_arrived(way, half - 1, ch)
@@ -532,7 +602,7 @@
     def adam(c, carry):
         at = pl.ds(pl.multiple_of(c * SLOT, SLOT), SLOT)
         grad = (
-            part[0, at]
+            part[at, :]
             + sum_in[0, half - 1, at].astype(F32)
             + sum_in[1, half - 1, at].astype(F32)
         )
@@ -546,10 +616,20 @@
 
     lax.fori_loop(0, rows // SLOT, adam, 0)
 
+    rows_arrived(3, dx_in)
+
+    def combine_dx(c, carry):
+        at = pl.ds(pl.multiple_of(c * block, block), block)
+        tokens_grad[:, at] = dot(place_t[...], dx_in[:, at], ((1,), (0,))).astype(BF16)
+        return carry
+
+    lax.fori_loop(0, width // block, combine_dx, 0)
+
     for n, ref in enumerate((x_send, g_send, ro_send, dx_send)):
         await_bytes(ref.at[pl.ds(0, others * SLOT)], a2a_s.at[n])
-    for a in range(2):
-        hops_sent(a)
+    hops_sent(0)
+    for a in (1, 2):
+        moment_hops_sent(a)
     for ch in range(CHUNKS):
         at = pl.ds(ch * part_rows, part_rows)
         for way in (0, 1):
@@ -617,7 +697,7 @@
             pltpu.VMEM((slots, width), BF16),
             pltpu.VMEM((2, half, rows, cols), BF16),
             pltpu.VMEM((2, half, rows, cols), BF16),
-            pltpu.VMEM((2, rows, cols), F32),
+            pltpu.VMEM((2 * rows, cols), F32),
             pltpu.VMEM((slots, tok), BF16),
             pltpu.VMEM((tok, slots), BF16),
             pltpu.VMEM((tok, slots), BF16),
@@ -627,19 +707,16 @@
             pltpu.VMEM((experts, SLOT, NARROW), BF16),
             pltpu.VMEM((experts, SLOT, WIDE), BF16),
             pltpu.VMEM((experts, SLOT, NARROW), BF16),
-            pltpu.VMEM((experts, 2, SLOT, WIDE), BF16),
-            pltpu.VMEM((experts, 2, SLOT, NARROW), BF16),
-            pltpu.VMEM((experts, 2, SLOT, WIDE), BF16),
-            pltpu.VMEM((experts, 2, SLOT, NARROW), BF16),
+            *[pltpu.VMEM((experts, SLOT, cols), BF16)] * 4,
             pltpu.VMEM((2, rows, cols), BF16),
             pltpu.VMEM((2, rows, cols), BF16),
             dma((2,)),
             dma((4,)),
             dma((4,)),
-            dma((2, 2)),
-            dma((2, 2)),
-            dma((2, 2)),
-            dma((2, 2)),
+            dma((3, 2)),
+            dma((3, 2)),
+            dma((3, 2)),
+            dma((3, 2)),
             dma((2, half, CHUNKS)),
             dma((2, half, CHUNKS)),
             dma((2, half, CHUNKS)),

time: 161 us -> 158 us (0.981)
  Pallas kernels: 153 us -> 149 us
    pallas_call x1, Pallas kernels: 153 us -> 149 us  [shards(): pl.pallas_call(functools.partial(kernel, (groups, experts, *grid)), out_s...]
where the time goes in v3:
time: 158 us
  Pallas kernels  149 us (94%)
  local copies, waits for them, and re-layouts  6.83 us (4%)
    pallas_call x1, Pallas kernels, shards(): pl.pallas_call(functools.partial(kernel, (groups, experts, *grid)), out_s...  149 us
    unnamed x20, local copies, waits for them, and re-layouts  6.83 us

profile of v3, /device:TPU:1, one launch (start us, length us, event | category | flops | bytes accessed | tf_op | source)
XLA Modules:
  0.0 157.5 jit_solution(3210081633015750943)
XLA Ops:
  0.6 0.0 copy-start.5
  0.6 0.0 copy-start.6
  0.7 0.6 copy-done.5
  1.3 0.0 copy-done.6
  1.3 0.6 select_reduce_fusion.source
  1.9 149.4 %moe_step.1 = (bf16[128,2048]{1,0:T(8,128)(2,1)}, bf16[128,2048]{1,0:T(8,128)(2,1)}, f32[3,128]{1,0:T(4,128)}, bf16[128,1152]{1,0:T(8,128)(2,1)}, bf16[128,1152]{1,0:T(8,128)(2,1)}, /*index=5*/bf16[128,1152]{1,0:T(8,128)(2,1)}) custom-call(s32[32]{0:T(128)} %select_reduce_fusion.source, bf16[128,2048]{1,0:T(8,128)(2,1)} %tokens.1, f32[3,128]{1,0:T(4,128)} %bitcast.16, ...), custom_call_target="tpu_custom_call" | custom-call | tf_op jit(solution)/shard_map/moe_step/pallas_call | solution.py:671
  151.3 0.0 copy-start
  151.3 1.9 %copy.21 = bf16[128,2048]{1,0:T(8,128)(2,1)} copy(bf16[128,2048]{1,0:T(8,128)(2,1)} %get-tuple-element.24) | data formatting | bytes 1048576
  153.3 0.0 copy-done
  153.3 0.0 copy-start.4
  153.3 0.0 copy-start.3
  153.3 0.8 copy.22
  154.1 0.0 copy-done.4
  154.1 0.6 copy.23
  154.7 0.0 copy-done.3
  154.7 0.0 copy-start.2
  154.7 0.7 copy.24
  155.4 0.4 copy-done.2
  155.7 0.0 copy-start.1
  155.7 0.7 copy.25
  156.4 0.4 copy-done.1
  156.8 0.7 copy.26
Async XLA Ops:
  0.6 0.7 copy-start.5
  0.6 0.7 copy-start.6
  151.3 2.0 %copy-start = (bf16[128,2048]{1,0:T(8,128)(2,1)S(1)}, bf16[128,2048]{1,0:T(8,128)(2,1)}, u32[]{:S(2)}) copy-start(bf16[128,2048]{1,0:T(8,128)(2,1)} %get-tuple-element.25) | copy-start | bytes 1572868
  153.3 0.8 copy-start.4
  153.3 1.4 copy-start.3
  154.7 1.1 copy-start.2
  155.7 1.1 copy-start.1

commit v4 on v3

--- a/solution.py
+++ b/solution.py
@@ -40,9 +40,10 @@
     moe_out,
     tokens_grad,
     gate_grads,
-    w_new,
-    m_new,
-    v_new,
+    grad_sum,
+    w_moved,
+    m_moved,
+    v_moved,
     x_send,
     g_send,
     x_in,
@@ -105,7 +106,7 @@
     low_bits = (1 << y_bits) - 1
 
     def peer(i):
-        off = (i * 11) & (experts - 1)
+        off = (i * 5) & (experts - 1)
         x_part = ((me >> y_bits) + (off >> y_bits)) & (xs - 1)
         y_part = ((me & low_bits & ~1) + (off & low_bits & ~1)) & low_bits
         return (x_part << y_bits) | y_part | ((me ^ off) & 1)
@@ -594,27 +595,18 @@
         )
     moment_arrived(1)
     moment_arrived(2)
+    w_moved[...] = weights[zone(dp), :]
+    m_moved[...] = moments[0]
+    v_moved[...] = moments[1]
     for ch in range(CHUNKS):
+        at = pl.ds(ch * part_rows, part_rows)
         for way in (0, 1):
             sum_arrived(way, half - 1, ch)
-    w_base = dp * rows
-
-    def adam(c, carry):
-        at = pl.ds(pl.multiple_of(c * SLOT, SLOT), SLOT)
-        grad = (
+        grad_sum[at, :] = (
             part[at, :]
             + sum_in[0, half - 1, at].astype(F32)
             + sum_in[1, half - 1, at].astype(F32)
         )
-        first = beta_one * moments[0, at].astype(F32) + (1.0 - beta_one) * grad
-        second = beta_two * moments[1, at].astype(F32) + (1.0 - beta_two) * grad * grad
-        old = weights[pl.ds(pl.multiple_of(w_base + c * SLOT, SLOT), SLOT), :].astype(F32)
-        w_new[at, :] = (old - learn_rate * first / (jnp.sqrt(second) + adam_eps)).astype(BF16)
-        m_new[at, :] = first.astype(BF16)
-        v_new[at, :] = second.astype(BF16)
-        return carry
-
-    lax.fori_loop(0, rows // SLOT, adam, 0)
 
     rows_arrived(3, dx_in)
 
@@ -674,6 +666,7 @@
             jax.ShapeDtypeStruct((tok, width), BF16),
             jax.ShapeDtypeStruct((tok, width), BF16),
             jax.ShapeDtypeStruct(route_gates.shape[::-1], F32),
+            jax.ShapeDtypeStruct((rows, cols), F32),
             state,
             state,
             state,
@@ -681,7 +674,7 @@
         in_specs=[pl.BlockSpec(memory_space=pltpu.SMEM)]
         + [vmem] * 6
         + [pl.BlockSpec(memory_space=pl.ANY)] * 2,
-        out_specs=(vmem,) * 6,
+        out_specs=(vmem,) * 7,
         scratch_shapes=[
             pltpu.VMEM((slots, width), BF16),
             pltpu.VMEM((slots, width), BF16),
@@ -737,8 +730,18 @@
         first_moment[0],
         second_moment[0],
     )
-    moe_out, tokens_grad, gate_grads, w_new, m_new, v_new = result
-    return (moe_out, tokens_grad, gate_grads.T, w_new[None], m_new[None], v_new[None])
+    moe_out, tokens_grad, gate_grads, grad, w_old, m_old, v_old = result
+    first = beta_one * m_old.astype(F32) + (1.0 - beta_one) * grad
+    second = beta_two * v_old.astype(F32) + (1.0 - beta_two) * grad * grad
+    w_new = w_old.astype(F32) - learn_rate * first / (jnp.sqrt(second) + adam_eps)
+    return (
+        moe_out,
+        tokens_grad,
+        gate_grads.T,
+        w_new.astype(BF16)[None],
+        first.astype(BF16)[None],
+        second.astype(BF16)[None],
+    )
 
 
 def solution(mesh):

time: 158 us -> 155 us (0.981)
  local copies, waits for them, and re-layouts: 6.83 us -> 3.27 us
  Pallas kernels: 149 us -> 146 us
  other arithmetic: 0.63 us -> 3.4 us
    unnamed x20 -> x13, local copies, waits for them, and re-layouts: 6.83 us -> 3.27 us
    pallas_call x1, Pallas kernels: 149 us -> 146 us  [shards(): pl.pallas_call(functools.partial(kernel, (groups, experts, *grid)), out_s...]
    broadcast_in_dim x0 -> x1, other arithmetic: none -> 2.77 us  [shards(): second.astype(BF16)[None]]
where the time goes in v4:
time: 155 us; the launch traced here: 154 us
  Pallas kernels  146 us (94%)
  other arithmetic  3.4 us (2%)
  local copies, waits for them, and re-layouts  3.27 us (2%)
    pallas_call x1, Pallas kernels, shards(): pl.pallas_call(functools.partial(kernel, (groups, experts, *grid)), out_s...  146 us
    unnamed x13, local copies, waits for them, and re-layouts  3.27 us

profile of v4, /device:TPU:1, one launch (start us, length us, event | category | flops | bytes accessed | tf_op | source)
XLA Modules:
  0.0 153.6 jit_solution(1970998407138574203)
XLA Ops:
  0.6 0.0 copy-start.3
  0.6 0.0 copy-start.4
  0.7 0.6 copy-done.3
  1.3 0.0 copy-done.4
  1.3 0.6 select_reduce_fusion.source
  1.9 146.3 %moe_step.1 = (bf16[128,2048]{1,0:T(8,128)(2,1)}, bf16[128,2048]{1,0:T(8,128)(2,1)}, f32[3,128]{1,0:T(4,128)}, f32[128,1152]{1,0:T(8,128)}, bf16[128,1152]{1,0:T...) custom-call(s32[32]{0:T(128)} %select_reduce_fusion.source, bf16[128,2048]{1,0:T(8,128)(2,1)} %tokens.1, ...), custom_call_target="tpu_custom_call" | custom-call | tf_op jit(solution)/shard_map/moe_step/pallas_call | solution.py:663
  148.2 0.0 copy-start.1
  148.2 2.8 %fusion.3 = (bf16[1,128,1152]{2,1,0:T(8,128)(2,1)}, bf16[1,128,1152]{2,1,0:T(8,128)(2,1)}, bf16[1,128,1152]{2,1,0:T(8,128)(2,1)}) fusion(f32[128,1152]{1,0:T(8,128)} %get-tuple-element.18, bf16[128,1152]{1,0:T(8,128)(2,1)} %get-tuple-element.19, bf16[128,1152]{1,0:T(8,128)(2,1)} %get-tuple-element.17, bf16[128,1152]{1,0:T(8,128)(2,1)} %get-tuple-element.16), kind=kLoop, calls=%fused_computation.6 | loop fusion | flops 2506752 | bytes 2359296 | tf_op jit(solution)/shard_map/broadcast_in_dim | solution.py:743
  151.0 0.0 copy-done.1
  151.0 0.0 copy-start
  151.0 0.8 copy.18
  151.8 0.4 copy-done
  152.2 0.0 copy-start.2
  152.2 0.8 copy.19
  153.0 0.0 copy-done.2
  153.0 0.6 copy.20
Async XLA Ops:
  0.6 0.7 copy-start.3
  0.6 0.7 copy-start.4
  148.2 2.8 %copy-start.1 = (bf16[128,2048]{1,0:T(8,128)(2,1)S(1)}, bf16[128,2048]{1,0:T(8,128)(2,1)}, u32[]{:S(2)}) copy-start(bf16[128,2048]{1,0:T(8,128)(2,1)} %get-tuple-element.29) | copy-start | bytes 1572868
  151.0 1.2 copy-start
  152.2 0.8 copy-start.2
